TPU v7x, 128 devices: a whole 4x4x4 slice. The times are simulated.
128 devices in a mesh: fsdp: 8 (over z, x_hi), ctx: 16 (over x_lo, y, core).
Axes of the slice: x: 4 (x_hi: 2, x_lo: 2; x = x_hi * 2 + x_lo), y: 4, z: 4, core: 2. Of those that a mesh axis runs over, the one named last changes fastest.
Arguments:
- hidden_in: bfloat16 [8, 2048, 2048], P('fsdp', 'ctx'), may hold values from -6 to 6
- out_grad: bfloat16 [8, 2048, 2048], P('fsdp', 'ctx'), may hold values from -6 to 6
- positions: int32 [8, 2048], P('fsdp', 'ctx'), may hold values from 0 to 6142, as said below
- documents: int32 [8, 2048], P('fsdp', 'ctx'), may hold values from 0 to 1, as said below
- qkv_weight: float32 [2048, 6144], P(('fsdp', 'ctx')), may hold values from -0.125 to 0.125
- qkv_first: float32 [2048, 6144], P(('fsdp', 'ctx')), may hold values from -80 to 80
- qkv_second: float32 [2048, 6144], P(('fsdp', 'ctx')), may hold values from 983.04 to 3276.8
- out_weight: float32 [2048, 2048], P(('fsdp', 'ctx')), may hold values from -0.5 to 0.5
- out_first: float32 [2048, 2048], P(('fsdp', 'ctx')), may hold values from -28 to 28
- out_second: float32 [2048, 2048], P(('fsdp', 'ctx')), may hold values from 117.9648 to 393.216
- gate_weight: float32 [2048, 5632], P(('fsdp', 'ctx')), may hold values from -0.125 to 0.125
- gate_first: float32 [2048, 5632], P(('fsdp', 'ctx')), may hold values from -28 to 28
- gate_second: float32 [2048, 5632], P(('fsdp', 'ctx')), may hold values from 127.7952 to 425.984
- up_weight: float32 [2048, 5632], P(('fsdp', 'ctx')), may hold values from -0.125 to 0.125
- up_first: float32 [2048, 5632], P(('fsdp', 'ctx')), may hold values from -28 to 28
- up_second: float32 [2048, 5632], P(('fsdp', 'ctx')), may hold values from 127.7952 to 425.984
- down_weight: float32 [5632, 2048], P(('fsdp', 'ctx')), may hold values from -0.078125 to 0.078125
- down_first: float32 [5632, 2048], P(('fsdp', 'ctx')), may hold values from -48 to 48
- down_second: float32 [5632, 2048], P(('fsdp', 'ctx')), may hold values from 353.8944 to 1179.648
- small_params: float32 [7, 2048], P(None, ('fsdp', 'ctx')), may hold values from -1 to 1.4, as said below
- small_first: float32 [7, 2048], P(None, ('fsdp', 'ctx')), may hold values from -80 to 80
- small_second: float32 [7, 2048], P(None, ('fsdp', 'ctx')), may hold values from 983.04 to 3276.8
Outputs:
- block_out: bfloat16 [8, 2048, 2048], P('fsdp', 'ctx')
- input_grad: float32 [8, 2048, 2048], P('fsdp', 'ctx')
- qkv_weight_new: float32 [2048, 6144], P(('fsdp', 'ctx'))
- qkv_first_new: float32 [2048, 6144], P(('fsdp', 'ctx'))
- qkv_second_new: float32 [2048, 6144], P(('fsdp', 'ctx'))
- out_weight_new: float32 [2048, 2048], P(('fsdp', 'ctx'))
- out_first_new: float32 [2048, 2048], P(('fsdp', 'ctx'))
- out_second_new: float32 [2048, 2048], P(('fsdp', 'ctx'))
- gate_weight_new: float32 [2048, 5632], P(('fsdp', 'ctx'))
- gate_first_new: float32 [2048, 5632], P(('fsdp', 'ctx'))
- gate_second_new: float32 [2048, 5632], P(('fsdp', 'ctx'))
- up_weight_new: float32 [2048, 5632], P(('fsdp', 'ctx'))
- up_first_new: float32 [2048, 5632], P(('fsdp', 'ctx'))
- up_second_new: float32 [2048, 5632], P(('fsdp', 'ctx'))
- down_weight_new: float32 [5632, 2048], P(('fsdp', 'ctx'))
- down_first_new: float32 [5632, 2048], P(('fsdp', 'ctx'))
- down_second_new: float32 [5632, 2048], P(('fsdp', 'ctx'))
- small_params_new: float32 [7, 2048], P(None, ('fsdp', 'ctx'))
- small_first_new: float32 [7, 2048], P(None, ('fsdp', 'ctx'))
- small_second_new: float32 [7, 2048], P(None, ('fsdp', 'ctx'))
Inputs may be any that keep to these rules, and one draw needn't show every extreme that they name: `documents`: each sequence holds document 0 on its first 1 to 127 positions and document 1 on all the rest. Within a document the positions rise by one; document 0 starts at a position below 4096, and document 1 ends at position 6142 in every sequence. `small_params`: gains lie in 0.6 to 1.4, shifts and biases in -1 to 1.
All inputs are finite; a program needn't handle non-finite values.
Results may differ from a plain program's by a relative error of at most 0.039.
Values may be sent and summed in bfloat16 or wider, within the bound.
A program may use at most 512 MiB of HBM per device.

v0:
```python
import functools
import math

import jax
import jax.numpy as jnp
import numpy as np
from jax import lax
from jax.experimental import pallas as pl
from jax.experimental.pallas import tpu as pltpu
from jax.sharding import Mesh
from jax.sharding import PartitionSpec as P

D = 2048
H = 32
HEAD = 64
FF = 5632
ROT = 16
STEP = 10

NORM_EPS = 1e-05
BETA_ONE = 0.9
BETA_TWO = 0.95
ADAM_EPS = 1e-08
MASKED = -1e30

AXES = ("z", "xh", "xl", "y", "core")
YC = ("y", "core")
ZX = ("z", "xh", "xl")
HALF = 1024
SEQ = 2048
BF = jnp.bfloat16
F32 = jnp.float32


def norm_forward(rows, gain, shift):
    mean = jnp.mean(rows, axis=-1, keepdims=True)
    centred = rows - mean
    scale = lax.rsqrt(jnp.mean(centred * centred, axis=-1, keepdims=True) + NORM_EPS)
    unit = centred * scale
    return (unit * gain + shift, unit, scale)


def norm_backward(gradient, unit, scale, gain):
    along = gradient * gain
    inner = (
        along
        - jnp.mean(along, axis=-1, keepdims=True)
        - unit * jnp.mean(along * unit, axis=-1, keepdims=True)
    )
    return (inner * scale, jnp.sum(gradient * unit, axis=0), jnp.sum(gradient, axis=0))


def adamw(weight, first, second, gradient, rate, decay):
    first_new = BETA_ONE * first + (1.0 - BETA_ONE) * gradient
    second_new = BETA_TWO * second + (1.0 - BETA_TWO) * gradient * gradient
    mean_hat = first_new / (1.0 - BETA_ONE**STEP)
    square_hat = second_new / (1.0 - BETA_TWO**STEP)
    weight_new = weight - rate * (mean_hat / (jnp.sqrt(square_hat) + ADAM_EPS) + decay * weight)
    return (weight_new, first_new, second_new)


def dot_nn(a, b):
    return jnp.dot(a, b, preferred_element_type=F32)


def dot_nt(a, b):
    return lax.dot_general(a, b, (((1,), (1,)), ((), ())), preferred_element_type=F32)


def dot_tn(a, b):
    return lax.dot_general(a, b, (((0,), (0,)), ((), ())), preferred_element_type=F32)


def document_marks(params_ref):
    sequence = lax.axis_index("z") * 2 + lax.axis_index("xh")
    row = params_ref[7:8, pl.ds(pl.multiple_of(sequence * 256, 128), 128)]
    lane = lax.broadcasted_iota(jnp.int32, (1, 128), 1)
    length, high, low = [
        jnp.sum(jnp.where(lane == k, row, 0.0), axis=1, keepdims=True) for k in range(3)
    ]
    return length, high * 64.0 + low


def rotary_angles(params_ref, half):
    length, start = document_marks(params_ref)
    place = lax.broadcasted_iota(jnp.int32, (8, HALF), 1).astype(F32) + half * float(HALF)
    position = jnp.where(place < length, start + place, 4095.0 + place)
    row = lax.broadcasted_iota(jnp.int32, (8, HALF), 0)
    freq = jnp.zeros((8, HALF), F32)
    for k in range(ROT // 2):
        freq = jnp.where(row == k, float(np.float32(10000.0) ** np.float32(-k / (ROT // 2))), freq)
    angle = position * freq
    parts = []
    for value in (jnp.cos(angle), jnp.sin(angle)):
        high = value.astype(BF).astype(F32)
        parts += [high, value - high]
    return jnp.concatenate(parts, axis=0).astype(BF)


def rotary_tables(angles):
    row = lax.broadcasted_iota(jnp.int32, (16, 128), 0) % 8
    lane = lax.broadcasted_iota(jnp.int32, (16, 128), 1) % HEAD
    spread = jnp.where((lane < ROT) & (lane % 8 == row), 1.0, 0.0).astype(BF)
    lane = lax.broadcasted_iota(jnp.int32, (1, 128), 1) % HEAD
    cosine = dot_tn(angles[0:16], spread) + jnp.where(lane < ROT, 0.0, 1.0)
    sine = dot_tn(angles[16:32], spread)
    return cosine, jnp.where(lane < ROT // 2, -sine, 0.0), jnp.where(lane < ROT // 2, 0.0, sine)


def rotate(x, cosine, below, above):
    return x * cosine + pltpu.roll(x, 120, 1) * below + pltpu.roll(x, 8, 1) * above


def remote(src, dst, sems, at, device):
    return pltpu.make_async_remote_copy(
        src_ref=src,
        dst_ref=dst,
        send_sem=sems.at[0, at],
        recv_sem=sems.at[1, at],
        device_id=device,
        device_id_type=pl.DeviceIdType.MESH,
    )


def places():
    y, c, z = lax.axis_index("y"), lax.axis_index("core"), lax.axis_index("z")
    x = lax.axis_index("xh") * 2 + lax.axis_index("xl")
    step = lambda v, k: lax.rem(v + k, 4)
    at_x = lambda v: {"xh": lax.div(v, 2), "xl": lax.rem(v, 2)}
    devices = {
        "twin": {"core": 1 - c},
        "up": {"y": step(y, 1)},
        "down": {"y": step(y, 3)},
        "across": {"y": step(y, 2)},
        "up_twin": {"y": step(y, 1), "core": 1 - c},
        "down_twin": {"y": step(y, 3), "core": 1 - c},
        "across_twin": {"y": step(y, 2), "core": 1 - c},
        "x+": at_x(step(x, 1)),
        "x-": at_x(step(x, 3)),
        "z+": {"z": step(z, 1)},
        "z-": {"z": step(z, 3)},
        "pair": {"xl": 1 - lax.axis_index("xl")},
    }
    return y, c, x, z, devices


def add_low(a, b):
    return (a.astype(F32) + b.astype(F32)).astype(BF)


class RingGather:
    def __init__(self, block, cut, i, plus, minus, sems, base, pending):
        self.lo, self.hi = cut(block(lax.rem(i + 3, 4)))[0], cut(block(lax.rem(i + 1, 4)))[1]
        self.to_plus = remote(block(i), block(i), sems, base, plus)
        self.to_minus = remote(block(i), block(i), sems, base + 1, minus)
        self.pass_plus = remote(self.lo, self.lo, sems, base + 2, plus)
        self.pass_minus = remote(self.hi, self.hi, sems, base + 3, minus)
        pending += [self.to_plus, self.to_minus, self.pass_plus, self.pass_minus]

    def start(self):
        self.to_plus.start()
        self.to_minus.start()

    def before_came(self):
        self.to_plus.wait_recv()
        self.pass_plus.start()

    def after_came(self):
        self.to_minus.wait_recv()
        self.pass_minus.start()

    def finish(self):
        self.pass_plus.wait_recv()
        self.pass_minus.wait_recv()


class RingSum:
    def __init__(self, blocks, cut, plus, minus, acc, near, sems, base, pending):
        across, after, before = blocks
        self.cut, self.after, self.before, self.acc, self.near = cut, after, before, acc, near
        send = lambda src, slot, which, at, device: remote(
            cut(src)[which], cut(near(slot))[which], sems, base + at, device
        )
        self.far_plus = send(across, 0, 0, 0, plus)
        self.far_minus = send(across, 0, 1, 1, minus)
        self.own_plus = send(after, 1, 1, 2, plus)
        self.own_minus = send(before, 2, 0, 3, minus)
        self.sum_plus = send(acc, 1, 0, 4, plus)
        self.sum_minus = send(acc, 2, 1, 5, minus)
        self.coming = [self.own_plus, self.own_minus, self.sum_plus, self.sum_minus]
        pending += [self.far_plus, self.far_minus] + self.coming

    def far(self):
        self.far_plus.start()
        self.far_minus.start()

    def own(self):
        self.own_plus.start()
        self.own_minus.start()

    def middle(self):
        near = self.near(0)
        self.far_plus.wait_recv()
        self.cut(self.acc)[0][...] = add_low(self.cut(self.after)[0][...], self.cut(near)[0][...])
        self.sum_plus.start()
        self.far_minus.wait_recv()
        self.cut(self.acc)[1][...] = add_low(self.cut(self.before)[1][...], self.cut(near)[1][...])
        self.sum_minus.start()

    def finish(self, mine):
        for copy in self.coming:
            copy.wait_recv()
        total = mine[...].astype(F32) + self.near(1)[...].astype(F32) + self.near(2)[...].astype(F32)
        return total.astype(BF)


def ring_gather(block, cut, i, plus, minus, sems, base, pending):
    before, after = lax.rem(i + 3, 4), lax.rem(i + 1, 4)
    to_plus = remote(block(i), block(i), sems, base, plus)
    to_minus = remote(block(i), block(i), sems, base + 1, minus)
    to_plus.start()
    to_minus.start()
    yield
    to_plus.wait_recv()
    lo = cut(block(before))[0]
    pass_plus = remote(lo, lo, sems, base + 2, plus)
    pass_plus.start()
    yield
    to_minus.wait_recv()
    hi = cut(block(after))[1]
    pass_minus = remote(hi, hi, sems, base + 3, minus)
    pass_minus.start()
    pending += [to_plus, to_minus, pass_plus, pass_minus]
    yield
    pass_plus.wait_recv()
    pass_minus.wait_recv()


def ring_scatter(block, cut, i, plus, minus, acc, near, sems, base, pending):
    before, after, across = lax.rem(i + 3, 4), lax.rem(i + 1, 4), lax.rem(i + 2, 4)
    lo, hi = (lambda v: cut(v)[0]), (lambda v: cut(v)[1])
    far_plus = remote(lo(block(across)), lo(near.at[0]), sems, base, plus)
    far_minus = remote(hi(block(across)), hi(near.at[0]), sems, base + 1, minus)
    own_plus = remote(hi(block(after)), hi(near.at[1]), sems, base + 2, plus)
    own_minus = remote(lo(block(before)), lo(near.at[2]), sems, base + 3, minus)
    for copy in (far_plus, far_minus, own_plus, own_minus):
        copy.start()
    yield
    far_plus.wait_recv()
    lo(acc)[...] = add_low(lo(block(after))[...], lo(near.at[0])[...])
    sum_plus = remote(lo(acc), lo(near.at[1]), sems, base + 4, plus)
    sum_plus.start()
    yield
    far_minus.wait_recv()
    hi(acc)[...] = add_low(hi(block(before))[...], hi(near.at[0])[...])
    sum_minus = remote(hi(acc), hi(near.at[2]), sems, base + 5, minus)
    sum_minus.start()
    pending += [far_plus, far_minus, own_plus, own_minus, sum_plus, sum_minus]
    yield
    for copy in (own_plus, own_minus, sum_plus, sum_minus):
        copy.wait_recv()


class GatherTokens:
    peers = ("twin", "up", "down")
    n_sems = 10

    def __init__(self, rows, width, normalize=False, far=False):
        self.ins = [((rows, width), BF, "far")] if far else [((rows, width), BF)]
        self.outs = [((8, rows, width), BF, "far")] if far else [((8, rows, width), BF)]
        self.scratch = [pltpu.VMEM((rows, width), BF)] if normalize else []
        self.rows = rows

    def run(self, ins, outs, scratch, sems, base, place, pending):
        y, c, _, _, to = place
        (x_ref,), (out_ref,) = ins, outs
        if scratch:
            rows = x_ref[...].astype(F32)
            centred = rows - jnp.mean(rows, axis=-1, keepdims=True)
            spread = jnp.mean(centred * centred, axis=-1, keepdims=True)
            (x_ref,) = scratch
            x_ref[...] = (centred * lax.rsqrt(spread + NORM_EPS)).astype(BF)
            yield
        half = self.rows // 2
        lo, hi = pl.ds(0, half), pl.ds(half, half)
        at = lambda k: lax.rem(y + k, 4) * 2 + c
        mine = pltpu.make_async_copy(x_ref, out_ref.at[at(0)], sems.at[0, base + 9])
        s_up = remote(x_ref, out_ref.at[at(0)], sems, base, to["up"])
        s_down = remote(x_ref, out_ref.at[at(0)], sems, base + 1, to["down"])
        s_twin = remote(x_ref, out_ref.at[at(0)], sems, base + 2, to["twin"])
        for copy in (s_up, s_down, s_twin, mine):
            copy.start()
        pass_on = lambda ref, k, device: remote(ref, ref, sems, base + k, to[device])
        yield
        s_up.wait_recv()
        r_up = pass_on(out_ref.at[at(3), lo], 3, "up")
        t_down = pass_on(out_ref.at[at(3)], 5, "twin")
        r_up.start()
        t_down.start()
        yield
        s_down.wait_recv()
        r_down = pass_on(out_ref.at[at(1), hi], 4, "down")
        t_up = pass_on(out_ref.at[at(1)], 6, "twin")
        r_down.start()
        t_up.start()
        yield
        r_up.wait_recv()
        t_lo = pass_on(out_ref.at[at(2), lo], 7, "twin")
        t_lo.start()
        yield
        r_down.wait_recv()
        t_hi = pass_on(out_ref.at[at(2), hi], 8, "twin")
        t_hi.start()
        pending += [s_up, s_down, s_twin, r_up, r_down, t_down, t_up, t_lo, t_hi]
        yield
        for copy in (s_twin, t_down, t_up, t_lo, t_hi):
            copy.wait_recv()
        mine.wait()


class SumTokens:
    peers = ("twin", "up", "down")
    n_sems = 10
    steps = (2, 1, 3, 0)

    def __init__(self, rows, width, plus=False):
        self.ins = [((8, rows, width), BF)] + [((rows, width), F32)] * plus
        self.outs = [((rows, width), BF if plus else F32)]
        self.scratch = [
            pltpu.VMEM((4, rows, width), BF),
            pltpu.VMEM((3, rows, width), BF),
            pltpu.VMEM((rows, width), BF),
            pltpu.VMEM((3, rows, width), BF),
        ]
        self.rows = rows

    def swap(self, k, p_ref, scratch, sems, base, place):
        y, c, _, _, to = place
        at = lax.rem(y + self.steps[k], 4) * 2
        copy = remote(p_ref.at[at + 1 - c], scratch[0].at[k], sems, base + k, to["twin"])
        copy.start()
        return copy

    def rest(self, swaps, p_ref, out_ref, extra, scratch, sems, base, place, pending):
        y, c, _, _, to = place
        from_twin, pair, acc, near = scratch
        half = self.rows // 2
        cut = lambda v: (v.at[pl.ds(0, half)], v.at[pl.ds(half, half)])

        def send(block, slot, which, at, device):
            copy = remote(cut(block)[which], cut(near.at[slot])[which], sems, base + at, to[device])
            copy.start()
            return copy

        for k, off in enumerate(self.steps[:3]):
            swaps[k].wait_recv()
            pair[k] = add_low(p_ref[lax.rem(y + off, 4) * 2 + c], from_twin[k])
            if k == 0:
                far_plus = send(pair.at[0], 0, 0, 4, "up")
                far_minus = send(pair.at[0], 0, 1, 5, "down")
            elif k == 1:
                own_plus = send(pair.at[1], 1, 1, 6, "up")
            else:
                own_minus = send(pair.at[2], 2, 0, 7, "down")
        yield
        far_plus.wait_recv()
        cut(acc)[0][...] = add_low(cut(pair.at[1])[0][...], cut(near.at[0])[0][...])
        sum_plus = send(acc, 1, 0, 8, "up")
        yield
        far_minus.wait_recv()
        cut(acc)[1][...] = add_low(cut(pair.at[2])[1][...], cut(near.at[0])[1][...])
        sum_minus = send(acc, 2, 1, 9, "down")
        swaps[3].wait_recv()
        total = p_ref[y * 2 + c].astype(F32) + from_twin[3].astype(F32)
        if extra is not None:
            total = total + extra[...]
        pending += list(swaps) + [far_plus, far_minus, own_plus, own_minus, sum_plus, sum_minus]
        yield
        for copy in (own_plus, own_minus, sum_plus, sum_minus):
            copy.wait_recv()
        total = total + (near[1].astype(F32) + near[2].astype(F32))
        out_ref[...] = total.astype(out_ref.dtype)

    def run(self, ins, outs, scratch, sems, base, place, pending):
        swaps = [self.swap(k, ins[0], scratch, sems, base, place) for k in range(4)]
        yield
        extra = ins[1] if len(ins) > 1 else None
        yield from self.rest(swaps, ins[0], outs[0], extra, scratch, sems, base, place, pending)


class LastRows:
    peers = SumTokens.peers
    n_sems = SumTokens.n_sems

    def __init__(self):
        self.sum = SumTokens(128, D)
        self.ins = [
            ((HALF, 768), BF),
            ((HALF, D), BF),
            ((D, 896), BF),
            ((128, D), BF),
            ((128, D), F32),
            ((16, D), F32),
        ]
        self.outs = [((128, D), F32)]
        self.scratch = [
            pltpu.VMEM((8, 128, D), BF),
            pltpu.VMEM((128, D), F32),
            pltpu.VMEM((8, D), F32),
            pltpu.VMEM((8, 768), F32),
        ] + self.sum.scratch

    def run(self, ins, outs, scratch, sems, base, place, pending):
        d_ref, u_ref, w_ref, x_ref, d_middle_ref, params_ref = ins
        p_ref, total_ref, norm_ref, bias_ref = scratch[:4]
        self.sums = norm_ref, bias_ref
        y, c = place[:2]
        norm_ref[...] = jnp.zeros_like(norm_ref)
        bias_ref[...] = jnp.zeros_like(bias_ref)

        def two_blocks(at):
            rows = pl.ds(pl.multiple_of(at * 128, 256), 256)
            d = d_ref[rows, :]
            dh = dot_nt(d, w_ref[:, 0:768])
            p_ref[pl.ds(at, 2)] = dh.astype(BF).reshape(2, 128, D)
            norm_ref[0:1] += jnp.sum(dh * u_ref[rows, :].astype(F32), axis=0, keepdims=True)
            norm_ref[1:2] += jnp.sum(dh, axis=0, keepdims=True)
            bias_ref[0:1] += jnp.sum(d.astype(F32), axis=0, keepdims=True)

        swaps = []
        for k, off in enumerate(self.sum.steps):
            at = lax.rem(y + off, 4) * 2
            two_blocks(at)
            swaps.append(self.sum.swap(k, p_ref, scratch[4:], sems, base, place))
            yield
        yield from self.sum.rest(
            swaps, p_ref, total_ref, None, scratch[4:], sems, base, place, pending
        )
        rows = x_ref[...].astype(F32)
        centred = rows - jnp.mean(rows, axis=-1, keepdims=True)
        scale = lax.rsqrt(jnp.mean(centred * centred, axis=-1, keepdims=True) + NORM_EPS)
        unit = centred * scale
        along = total_ref[...] * params_ref[0:1]
        inner = (
            along
            - jnp.mean(along, axis=-1, keepdims=True)
            - unit * jnp.mean(along * unit, axis=-1, keepdims=True)
        )
        outs[0][...] = d_middle_ref[...] + inner * scale


def rows_or_columns(rows, width):
    if rows % 32 == 0:
        return lambda v: (v.at[pl.ds(0, rows // 2)], v.at[pl.ds(rows // 2, rows // 2)])
    return lambda v: (v.at[:, pl.ds(0, width // 2)], v.at[:, pl.ds(width // 2, width // 2)])


class GatherWeights:
    peers = ("x+", "x-", "z+", "z-")
    n_sems = 41

    def __init__(self, rows, width):
        self.ins = [((rows, width), BF)]
        self.outs = [((4, 4, rows, width), BF)]
        self.scratch = []
        self.rows, self.width = rows, width

    def rings(self, out_ref, sems, base, place, pending):
        _, _, x, z, to = place
        first = self.width // 256 * 128

        def one(order, base):
            width = self.width - first if order else first
            part = pl.ds(order * first, width)
            cut = rows_or_columns(self.rows, width)
            if order == 0:
                block = lambda k, j: out_ref.at[k, j, pl.ds(0, self.rows), part]
                i, k, ring, other = x, z, (to["x+"], to["x-"]), (to["z+"], to["z-"])
            else:
                block = lambda k, j: out_ref.at[j, k, pl.ds(0, self.rows), part]
                i, k, ring, other = z, x, (to["z+"], to["z-"]), (to["x+"], to["x-"])
            main = RingGather(lambda j: block(k, j), cut, i, *ring, sems, base, pending)
            mine, after, across, before = [
                RingGather(
                    lambda q, j=lax.rem(i + n, 4): block(q, j), cut, k, *other, sems, base + 4 + 4 * n, pending
                )
                for n in range(4)
            ]
            main.start()
            mine.start()
            yield
            main.before_came()
            before.start()
            yield
            main.after_came()
            after.start()
            yield
            mine.before_came()
            mine.after_came()
            yield
            main.finish()
            across.start()
            yield
            for part_ring in (before, after):
                part_ring.before_came()
                part_ring.after_came()
            yield
            across.before_came()
            across.after_came()
            yield
            for part_ring in (mine, before, after, across):
                part_ring.finish()

        yield from both(one(0, base), one(1, base + 20))

    def run(self, ins, outs, scratch, sems, base, place, pending):
        _, _, x, z, _ = place
        (x_ref,), (out_ref,) = ins, outs
        mine = pltpu.make_async_copy(x_ref, out_ref.at[z, x], sems.at[0, base + 40])
        mine.start()
        mine.wait()
        yield from self.rings(out_ref, sems, base, place, pending)


class SumWeights:
    peers = ("x+", "x-", "z+", "z-")
    n_sems = 60

    def __init__(self, rows, width):
        self.ins = [((4, 4, rows, width), BF)]
        self.outs = [((rows, width), BF)]
        self.rows, self.width = rows, width
        first = width // 256 * 128
        self.widths = (first, width - first)
        self.scratch = []
        for w in self.widths:
            self.scratch += [
                pltpu.VMEM((4, rows, w), BF),
                pltpu.VMEM((3, 4, rows, w), BF),
                pltpu.VMEM((4, rows, w), BF),
                pltpu.VMEM((rows, w), BF),
                pltpu.VMEM((3, rows, w), BF),
            ]

    def run(self, ins, outs, scratch, sems, base, place, pending):
        _, _, x, z, to = place
        (p_ref,), (out_ref,) = ins, outs
        every = pl.ds(0, self.rows)

        def one(order, bufs, base):
            acc, near, total, acc_two, near_two = bufs
            width = self.widths[order]
            part = pl.ds(order * self.widths[0], width)
            cut = rows_or_columns(self.rows, width)
            if order == 0:
                block = lambda k, j: p_ref.at[k, j, every, part]
                i, k, ring, other = x, z, (to["x+"], to["x-"]), (to["z+"], to["z-"])
            else:
                block = lambda k, j: p_ref.at[j, k, every, part]
                i, k, ring, other = z, x, (to["z+"], to["z-"]), (to["x+"], to["x-"])
            firsts = []
            for n, off in enumerate((2, 1, 3, 0)):
                at = lax.rem(k + off, 4)
                blocks = [block(at, lax.rem(i + m, 4)) for m in (2, 1, 3)]
                firsts.append(
                    RingSum(
                        blocks, cut, *ring, acc.at[n], lambda s, n=n: near.at[s, n], sems, base + 6 * n, pending
                    )
                )
            second = RingSum(
                [total.at[n] for n in range(3)], cut, *other, acc_two, lambda s: near_two.at[s], sems,
                base + 24, pending,
            )

            def complete(n):
                total[n] = firsts[n].finish(block(lax.rem(k + (2, 1, 3, 0)[n], 4), i))

            for one_ring in firsts:
                one_ring.far()
                one_ring.own()
            yield
            firsts[0].middle()
            firsts[1].middle()
            yield
            firsts[2].middle()
            firsts[3].middle()
            yield
            complete(0)
            second.far()
            yield
            complete(1)
            complete(2)
            second.own()
            yield
            second.middle()
            complete(3)
            yield
            out_ref[every, part] = second.finish(total.at[3])

        yield from both(one(0, scratch[:5], base), one(1, scratch[5:], base + 30))


def firsts(v):
    return v.at[pl.ds(0, 2)], v.at[pl.ds(2, 2)]


class GatherSmall:
    peers = ("x+", "x-", "z+", "z-")
    n_sems = 17

    def __init__(self, rows, width):
        self.ins = [((rows, width), BF)]
        self.outs = [((4, 4, rows, width), BF)]
        self.scratch = []
        self.rows, self.width = rows, width

    def rings(self, out_ref, sems, base, place, pending):
        _, _, x, z, to = place
        first = self.width // 256 * 128
        a, b = pl.ds(0, first), pl.ds(first, self.width - first)
        every = pl.ds(0, self.rows)
        cut_a = rows_or_columns(self.rows, first)
        cut_b = rows_or_columns(self.rows, self.width - first)

        def along_x_first():
            yield from ring_gather(
                lambda j: out_ref.at[z, j, every, a], cut_a, x, to["x+"], to["x-"], sems, base, pending
            )
            yield from ring_gather(
                lambda j: out_ref.at[j, pl.ds(0, 4), every, a], firsts, z, to["z+"], to["z-"], sems, base + 4,
                pending,
            )

        def along_z_first():
            yield from ring_gather(
                lambda j: out_ref.at[j, x, every, b], cut_b, z, to["z+"], to["z-"], sems, base + 8, pending
            )
            yield from ring_gather(
                lambda j: out_ref.at[pl.ds(0, 4), j, every, b], firsts, x, to["x+"], to["x-"], sems,
                base + 12, pending,
            )

        yield from both(along_x_first(), along_z_first())

    def run(self, ins, outs, scratch, sems, base, place, pending):
        _, _, x, z, _ = place
        (x_ref,), (out_ref,) = ins, outs
        mine = pltpu.make_async_copy(x_ref, out_ref.at[z, x], sems.at[0, base + 16])
        mine.start()
        mine.wait()
        yield from self.rings(out_ref, sems, base, place, pending)


class SumFew:
    peers = ("x+", "x-", "z+", "z-")
    n_sems = 24

    def __init__(self, rows, width):
        self.ins = [((4, 4, rows, width), BF)]
        self.outs = [((rows, width), BF)]
        self.rows, self.width = rows, width
        first = width // 256 * 128
        self.widths = (first, width - first)
        self.scratch = []
        for w in self.widths:
            self.scratch += [
                pltpu.VMEM((4, rows, w), BF),
                pltpu.VMEM((3, 4, rows, w), BF),
                pltpu.VMEM((4, rows, w), BF),
                pltpu.VMEM((rows, w), BF),
                pltpu.VMEM((3, rows, w), BF),
            ]

    def run(self, ins, outs, scratch, sems, base, place, pending):
        _, _, x, z, to = place
        (p_ref,), (out_ref,) = ins, outs
        every = pl.ds(0, self.rows)

        def one(order, bufs, base):
            acc, near, total, acc_two, near_two = bufs
            width = self.widths[order]
            columns = pl.ds(order * self.widths[0], width)
            cut = rows_or_columns(self.rows, width)
            four = pl.ds(0, 4)
            if order == 0:
                block = lambda j: p_ref.at[four, j, every, columns]
                i, k, far, close = x, z, ("x+", "x-"), ("z+", "z-")
            else:
                block = lambda j: p_ref.at[j, four, every, columns]
                i, k, far, close = z, x, ("z+", "z-"), ("x+", "x-")
            yield from ring_scatter(
                block, firsts, i, to[far[0]], to[far[1]], acc, near, sems, base, pending
            )
            total[...] = (
                block(i)[...].astype(F32) + near[1].astype(F32) + near[2].astype(F32)
            ).astype(BF)
            yield from ring_scatter(
                lambda j: total.at[j], cut, k, to[close[0]], to[close[1]], acc_two, near_two, sems,
                base + 6, pending,
            )
            out_ref[every, columns] = (
                total[k].astype(F32) + near_two[1].astype(F32) + near_two[2].astype(F32)
            ).astype(BF)

        yield from both(one(0, scratch[:5], base), one(1, scratch[5:], base + 12))


class Swap:
    peers = ("twin", "up", "down", "across", "up_twin", "down_twin", "across_twin")
    n_sems = 8
    steps = ((0, 1), (1, 0), (3, 0), (2, 0), (1, 1), (3, 1), (2, 1))

    def __init__(self, rows, width):
        self.ins = [((8, rows, width), BF)]
        self.outs = [((8, rows, width), BF)]
        self.scratch = []

    def send(self, x_ref, out_ref, sems, base, place):
        y, c, _, _, to = place
        me = y * 2 + c
        copies = [pltpu.make_async_copy(x_ref.at[me], out_ref.at[me], sems.at[0, base + 7])]
        for k, (name, (up, other)) in enumerate(zip(self.peers, self.steps)):
            at = lax.rem(y + up, 4) * 2 + (1 - c if other else c)
            copies.append(remote(x_ref.at[at], out_ref.at[me], sems, base + k, to[name]))
        for copy in copies:
            copy.start()
        return copies

    def run(self, ins, outs, scratch, sems, base, place, pending):
        copies = self.send(ins[0], outs[0], sems, base, place)
        yield
        copies[0].wait()
        for copy in copies[1:]:
            copy.wait_recv()
        pending += copies[1:]


def columns(at, width):
    return slice(at, at + width)


class ShareQkv:
    peers = Swap.peers + GatherWeights.peers

    def __init__(self):
        self.swap = Swap(16, 896)
        self.gather = GatherWeights(128, 896)
        self.ins = [((16, 6144), F32, "far"), ((16, 128), BF)]
        self.outs = [(*self.gather.outs[0], "far"), ((16, 16 * 128), F32)]
        self.scratch = [pltpu.VMEM((8, 16, 896), BF)] * 2
        self.n_sems = 16 + self.gather.n_sems

    def run(self, ins, outs, scratch, sems, base, place, pending):
        _, _, x, z, _ = place
        weight_ref, tile_ref = ins
        (out_ref, tiles_ref), (piece, landed) = outs, scratch
        for k in range(8):
            for pair in range(2):
                for kind in range(3):
                    piece[k, :, columns(pair * 384 + kind * 128, 128)] = weight_ref[
                        :, columns(kind * D + k * 256 + pair * 128, 128)
                    ].astype(BF)
            piece[k, :, columns(768, 128)] = tile_ref[...]
        yield from self.swap.run((piece,), (landed,), (), sems, base, place, pending)
        for k in range(8):
            out_ref[z, x, columns(k * 16, 16)] = landed[k]
        yield from self.gather.rings(out_ref, sems, base + 16, place, pending)
        for k in range(16):
            tiles = [
                out_ref[k // 4, k % 4, columns(j * 16, 16), columns(768, 128)].astype(F32)
                for j in range(8)
            ]
            tiles_ref[:, columns(k * 128, 128)] = sum(tiles[1:], tiles[0])


def moved(read, tile, pieces, last):
    lane = lax.broadcasted_iota(jnp.int32, (16, 128), 1)
    value = jnp.zeros((16, 128), F32)
    for there, source, here, width in pieces:
        at = there - tile * 128
        if at + width <= 0 or at >= 128:
            continue
        start = min(here // 128 * 128, last)
        window = read(source, columns(start, 256)).astype(F32)
        shift = (at - (here - start)) % 256
        window = (pltpu.roll(window, shift, 1) if shift else window)[:, 0:128]
        value = jnp.where((lane >= at) & (lane < at + width), window, value)
    return value


class ShareHidden:
    peers = Swap.peers

    def __init__(self):
        self.swap = Swap(16, 1536)
        self.ins = [((16, FF), F32, "far")] * 2
        self.outs = self.swap.outs
        self.scratch = [pltpu.VMEM((8, 16, 1536), BF)]
        self.n_sems = self.swap.n_sems

    def run(self, ins, outs, scratch, sems, base, place, pending):
        (piece,) = scratch
        for k in range(8):
            pieces = [(j * 48, None, (j * 8 + k) * 44, 44) for j in range(16)]
            for w, ref in enumerate(ins):
                for tile in range(6):
                    value = moved(lambda _, at: ref[:, at], tile, pieces, FF - 256)
                    piece[k, :, columns(w * 768 + tile * 128, 128)] = value.astype(BF)
            yield
        yield from self.swap.run((piece,), outs, (), sems, base, place, pending)


class TokenSums:
    peers = ()
    n_sems = 0

    def __init__(self, rows, width, count, step=256):
        self.ins = [((HALF, rows), BF)] + [((HALF, width), BF)] * count
        self.outs = [((rows, width), BF)] * count
        self.scratch = []
        self.steps = [pl.ds(k, step) for k in range(0, rows, step)]

    def run(self, ins, outs, scratch, sems, base, place, pending):
        for columns in self.steps:
            for b_ref, out_ref in zip(ins[1:], outs):
                out_ref[columns, :] = dot_tn(ins[0][:, columns], b_ref[...]).astype(BF)
            yield


class GradThenSum:
    peers = SumWeights.peers

    def __init__(self, rows, width, steps, swap=False):
        self.sum = SumWeights(rows // 16, width)
        self.swap = Swap(rows // 128, width) if swap else None
        self.ins = [((HALF, rows), BF), ((HALF, width), BF)]
        self.outs = self.swap.outs if swap else self.sum.outs
        self.scratch = [pltpu.VMEM((4, 4, rows // 16, width), BF)] + self.sum.scratch
        self.n_sems = self.sum.n_sems
        if swap:
            self.peers = Swap.peers + SumWeights.peers
            self.scratch += [pltpu.VMEM((rows // 16, width), BF), pltpu.VMEM((8, rows // 128, width), BF)]
            self.n_sems += 8
        self.rows, self.steps = rows, steps

    def run(self, ins, outs, scratch, sems, base, place, pending):
        terms = scratch[0]
        block, step = self.rows // 16, self.rows // self.steps
        for k in range(self.steps):
            part = dot_tn(ins[0][:, columns(k * step, step)], ins[1][...]).astype(BF)
            for j in range(step // block):
                at = k * step // block + j
                terms[at // 4, at % 4] = part[columns(j * block, block)]
            yield
        if self.swap is None:
            yield from self.sum.run((terms,), outs, scratch[1:], sems, base, place, pending)
            return
        *buffers, total, piece = scratch[1:]
        yield from self.sum.run((terms,), (total,), buffers, sems, base, place, pending)
        count = self.rows // 128
        for k in range(8):
            piece[k] = total[columns(k * count, count)]
        at = base + self.sum.n_sems
        yield from self.swap.run((piece,), outs, (), sems, at, place, pending)


class Product:
    peers = ()
    n_sems = 0

    def __init__(self, depth, width):
        self.ins = [((HALF, depth), BF), ((depth, width), BF)]
        self.outs = [((HALF, width), BF)]
        self.scratch = []

    def run(self, ins, outs, scratch, sems, base, place, pending):
        for k in range(0, HALF, 256):
            outs[0][pl.ds(k, 256), :] = dot_nn(ins[0][pl.ds(k, 256), :], ins[1][...]).astype(BF)
            yield


class SumSmall:
    peers = Swap.peers + SumFew.peers

    def __init__(self, last):
        self.last = last
        self.swap = Swap(16, 512)
        self.sum = SumFew(16, 512)
        self.ins = [((8, D), F32)]
        self.outs = self.sum.outs
        self.scratch = [
            pltpu.VMEM((8, 16, 512), F32),
            pltpu.VMEM((8, 16, 512), BF),
            pltpu.VMEM((8, 16, 512), BF),
            pltpu.VMEM((4, 4, 16, 512), BF),
        ] + self.sum.scratch
        self.n_sems = 8 + self.sum.n_sems

    def run(self, ins, outs, scratch, sems, base, place, pending):
        wide, piece, landed, spread = scratch[:4]
        norm_ref, bias_ref = self.last.sums
        yc = place[0] * 2 + place[1]
        wide[...] = jnp.zeros_like(wide)
        for k in range(8):
            at = columns(k * 256, 256)
            wide[k, 0:8, 0:256] = ins[0][:, at]
            wide[k, 0:2, 0:256] = norm_ref[0:2, at]
        for pair in range(2):
            for kind in range(3):
                wide[yc, 2 + kind : 3 + kind, columns(pair * 128, 128)] = bias_ref[
                    0:1, columns((pair * 3 + kind) * 128, 128)
                ]
        piece[...] = wide[...].astype(BF)
        yield from self.swap.run((piece,), (landed,), (), sems, base, place, pending)
        total = jnp.sum(landed[...].astype(F32), axis=0).astype(BF)
        spread[...] = jnp.broadcast_to(total[None, None], spread.shape)
        yield from self.sum.run((spread,), outs, scratch[4:], sems, base + 8, place, pending)


def both(*parts):
    parts = list(parts)
    while parts:
        for part in list(parts):
            try:
                next(part)
            except StopIteration:
                parts.remove(part)
        yield


def in_order(parts, order):
    for letter in order:
        next(parts["abcdef".index(letter)], None)
    for _ in both(*parts):
        pass


def size(shape, dtype):
    return math.prod(shape) * jnp.dtype(dtype).itemsize


def loaded(part, copies):
    for copy in copies:
        copy.wait()
    yield from part


def stored(part, copies):
    yield from part
    for copy in copies:
        copy.start()


def comm_kernel(parts, order, *refs):
    *refs, sems, move_sems = refs
    refs = list(refs)
    take = lambda count: [refs.pop(0) for _ in range(count)]
    ins = [take(len(p.ins)) for p in parts]
    outs = [take(len(p.outs)) for p in parts]
    scratch = [take(len(p.scratch)) for p in parts]
    loads, stores, moves = [], [], 0
    for p, p_ins, p_outs in zip(parts, ins, outs):
        for refs_of, specs, copies in ((p_ins, p.ins, loads), (p_outs, p.outs, stores)):
            copies.append([])
            for k, spec in enumerate(specs):
                if len(spec) > 2:
                    far, near = refs_of[k], refs.pop(0)
                    ends = (far, near) if copies is loads else (near, far)
                    copies[-1].append(pltpu.make_async_copy(*ends, move_sems.at[moves]))
                    moves += 1
                    refs_of[k] = near
    for copy in sum(loads, []):
        copy.start()
    place = places()
    names = []
    for p in parts:
        names += [n for n in p.peers if n not in names]
    barrier = pltpu.get_barrier_semaphore()
    for name in names:
        pl.semaphore_signal(
            barrier, inc=1, device_id=place[4][name], device_id_type=pl.DeviceIdType.MESH
        )
    pl.semaphore_wait(barrier, len(names))
    base, running, pending = 0, [], []
    for k, p in enumerate(parts):
        p.held = outs[k]
        steps = p.run(ins[k], outs[k], scratch[k], sems, base, place, pending)
        running.append(stored(loaded(steps, loads[k]), stores[k]))
        base += p.n_sems
    in_order(running, order)
    for copy in pending:
        copy.wait_send()
    for copy in sum(stores, []):
        copy.wait()


def comm(collective_id, order, *pairs):
    parts = [p for p, _ in pairs]
    operands = [x.reshape(spec[0]) for p, xs in pairs for x, spec in zip(xs, p.ins)]
    operands = [
        pltpu.with_memory_space_constraint(x, pltpu.HBM) if len(spec) > 2 else x
        for x, spec in zip(operands, [spec for p in parts for spec in p.ins])
    ]
    in_specs = [spec for p in parts for spec in p.ins]
    out_specs = [spec for p in parts for spec in p.outs]
    marked = [spec for p in parts for spec in (*p.ins, *p.outs) if len(spec) > 2]
    where = lambda spec: pl.BlockSpec(memory_space=pltpu.HBM if len(spec) > 2 else pltpu.VMEM)
    held = sum(size(*spec[:2]) for spec in in_specs + out_specs)
    held += sum(size(s.shape, s.dtype) for p in parts for s in p.scratch)
    sent = sum(math.prod(spec[0]) for spec in out_specs) * 2
    return pl.pallas_call(
        functools.partial(comm_kernel, parts, order),
        out_shape=[(pltpu.HBM if len(spec) > 2 else jax.ShapeDtypeStruct)(*spec[:2]) for spec in out_specs],
        in_specs=[where(spec) for spec in in_specs],
        out_specs=[where(spec) for spec in out_specs],
        scratch_shapes=[s for p in parts for s in p.scratch]
        + [pltpu.VMEM(*spec[:2]) for spec in marked]
        + [
            pltpu.SemaphoreType.DMA((2, sum(p.n_sems for p in parts))),
            pltpu.SemaphoreType.DMA((max(1, len(marked)),)),
        ],
        compiler_params=pltpu.CompilerParams(
            collective_id=collective_id, has_side_effects=True, vmem_limit_bytes=held + (8 << 20)
        ),
        cost_estimate=pl.CostEstimate(flops=0, bytes_accessed=20 * sent, transcendentals=0),
    )(*operands)


ROWS = 256


class MakeQkv:
    peers = ()
    n_sems = 0

    def __init__(self, weights, units):
        self.weights, self.units = weights, units
        self.ins = []
        self.outs = [((HALF, D), BF), ((HALF, 768), BF), ((2, 32, HALF), BF)]
        self.scratch = []

    def run(self, ins, outs, scratch, sems, base, place, pending):
        h_ref, out_ref, angles_ref = outs
        w_ref, params_ref = self.weights.held
        (u_ref,) = self.units.held
        yc = place[0] * 2 + place[1]
        xl = lax.axis_index("xl")
        for half in range(2):
            angles_ref[half] = rotary_angles(params_ref, half)
        weight = w_ref[:, :, :, 0:768].reshape(D, 768)
        for k in range(4):
            rows = columns(k * ROWS, ROWS)
            unit = u_ref[2 * k : 2 * k + 2].reshape(ROWS, D).astype(F32)
            h = (unit * params_ref[0:1] + params_ref[1:2]).astype(BF)
            h_ref[rows, :] = h
            mixed = dot_nn(h, weight)
            tables = rotary_tables(angles_ref[xl, :, rows])
            for j in range(6):
                pair, kind = j // 3, j % 3
                at = pl.ds(pl.multiple_of(yc * 256 + pair * 128, 128), 128)
                part = mixed[:, columns(j * 128, 128)] + params_ref[2 + kind : 3 + kind, at]
                if kind < 2:
                    part = rotate(part, *tables)
                out_ref[rows, columns(j * 128, 128)] = part.astype(BF)
        yield


def rowwise(width):
    return pl.BlockSpec((ROWS, width), lambda i: (i, 0))


def fixed(*shape):
    return pl.BlockSpec(shape, lambda i: (0,) * len(shape), pipeline_mode=pl.Buffered(1))


BLOCK = 512
Q, K, V = slice(0, 128), slice(128, 256), slice(256, 384)


def only(x, h):
    lane = lax.broadcasted_iota(jnp.int32, (1, 128), 1)
    return jnp.where((lane >= h * HEAD) & (lane < (h + 1) * HEAD), x, jnp.zeros_like(x))


def rows_of(k):
    return slice(k * BLOCK, (k + 1) * BLOCK)


def allowed_mask(first_len, key_half, kb, query_half, qb, diagonal):
    key = lax.broadcasted_iota(jnp.int32, (BLOCK, BLOCK), 0) + kb * BLOCK
    query = lax.broadcasted_iota(jnp.int32, (BLOCK, BLOCK), 1) + qb * BLOCK
    allowed = None
    if diagonal and kb == qb:
        allowed = key <= query
    if kb == 0:
        length = first_len.astype(jnp.int32)
        same = (key + key_half * HALF >= length) | (query + query_half * HALF < length)
        allowed = same if allowed is None else allowed & same
    return allowed


def lanes(at, width):
    return pl.ds(pl.multiple_of(at * width, 128), width)


class Attend:
    peers = ("pair",)
    n_sems = 6

    def __init__(self):
        self.ins = [((16, D), F32), ((HALF, 768), BF)]
        self.outs = [
            ((HALF, 256), BF),
            ((2, 128, HALF), F32),
            ((2, 8, HALF), F32),
            ((2, HALF, 384), BF),
        ]
        self.scratch = [pltpu.VMEM((2, 8, HALF), F32), pltpu.VMEM((2, HALF, 128), BF)]

    def run(self, ins, outs, scratch, sems, base, place, pending):
        params_ref, qkv_ref = ins
        o_ref, acc_ref, top_ref, x_ref = outs
        total_ref, half_ref = scratch
        pair = place[4]["pair"]
        xl = lax.axis_index("xl")
        first_len = document_marks(params_ref)[0]
        sent = []
        for b in range(2):
            copy = remote(
                qkv_ref.at[rows_of(b), lanes(1 - xl, 384)], x_ref.at[xl, rows_of(b)], sems, base + b, pair
            )
            copy.start()
            sent.append(copy)
        kept = pltpu.make_async_copy(qkv_ref.at[:, lanes(xl, 384)], x_ref.at[xl], sems.at[0, base + 2])
        kept.start()
        kept.wait()
        yield

        def block(query_half, key_half, qb, h, state, diagonal):
            qs = rows_of(qb)
            qh = only(x_ref[query_half, qs, Q] * jnp.asarray(HEAD**-0.5, BF), h)
            top, total, acc = state
            for kb in range(qb + 1 if diagonal else 2):
                ks = rows_of(kb)
                scores = dot_nt(x_ref[key_half, ks, K], qh)
                allowed = allowed_mask(first_len, key_half, kb, query_half, qb, diagonal)
                if allowed is not None:
                    scores = jnp.where(allowed, scores, MASKED)
                new_top = jnp.maximum(top, jnp.max(scores, axis=0, keepdims=True))
                weights = jnp.exp(scores - new_top)
                if allowed is not None:
                    weights = jnp.where(allowed, weights, 0.0)
                shrink = jnp.exp(top - new_top)
                total = total * shrink + jnp.sum(weights, axis=0, keepdims=True)
                part = dot_tn(only(x_ref[key_half, ks, V], h), weights.astype(BF))
                acc = acc * shrink + part[h * HEAD : (h + 1) * HEAD]
                top = new_top
            top_ref[query_half, h : h + 1, qs] = top
            total_ref[query_half, h : h + 1, qs] = total
            acc_ref[query_half, h * HEAD : (h + 1) * HEAD, qs] = acc

        def diagonal(half):
            for qb in range(2):
                for h in range(2):
                    start = (
                        jnp.full((1, BLOCK), MASKED, F32),
                        jnp.zeros((1, BLOCK), F32),
                        jnp.zeros((HEAD, BLOCK), F32),
                    )
                    block(half, half, qb, h, start, True)

        def finish(half):
            for qb in range(2):
                qs = rows_of(qb)
                for h in range(2):
                    hs = slice(h * HEAD, (h + 1) * HEAD)
                    total = total_ref[half, h : h + 1, qs]
                    acc_ref[half, hs, qs] = acc_ref[half, hs, qs] / total
                    top_ref[half, h : h + 1, qs] = top_ref[half, h : h + 1, qs] + jnp.log(total)
                half_ref[half, qs, :] = acc_ref[half, :, qs].T.astype(BF)

        diagonal(xl)
        yield
        for copy in sent:
            copy.wait_recv()
        diagonal(1 - xl)
        yield
        for qb in range(2):
            for h in range(2):
                qs = rows_of(qb)
                state = (
                    top_ref[1, h : h + 1, qs],
                    total_ref[1, h : h + 1, qs],
                    acc_ref[1, h * HEAD : (h + 1) * HEAD, qs],
                )
                block(1, 0, qb, h, state, False)
            yield
        finish(1 - xl)
        back = remote(half_ref.at[1 - xl], o_ref.at[:, lanes(xl, 128)], sems, base + 3, pair)
        back.start()
        finish(xl)
        mine = pltpu.make_async_copy(half_ref.at[xl], o_ref.at[:, lanes(xl, 128)], sems.at[0, base + 4])
        mine.start()
        pending += sent + [back]
        yield
        mine.wait()
        back.wait_recv()


class AttendBack:
    peers = ("pair",)
    n_sems = 6

    def __init__(self):
        self.ins = [
            ((16, D), F32),
            ((2, HALF, 384), BF),
            ((HALF, 256), BF),
            ((2, 128, HALF), F32),
            ((2, 8, HALF), F32),
            ((2, 32, HALF), BF),
        ]
        self.outs = [((HALF, 768), BF)]
        self.scratch = [
            pltpu.VMEM((2, HALF, 128), BF),
            pltpu.VMEM((2, 128, HALF), F32),
            pltpu.VMEM((2, HALF, 128), F32),
            pltpu.VMEM((2, HALF, 128), F32),
            pltpu.VMEM((2, HALF, 384), BF),
        ]

    def run(self, ins, outs, scratch, sems, base, place, pending):
        params_ref, x_ref, own_ref, ot_ref, lse_ref, angles_ref = ins
        (out_ref,) = outs
        do_ref, dqt_ref, dk_ref, dv_ref, half_ref = scratch
        pair = place[4]["pair"]
        xl = lax.axis_index("xl")
        first_len = document_marks(params_ref)[0]
        sent = remote(own_ref.at[:, lanes(1 - xl, 128)], do_ref.at[xl], sems, base, pair)
        sent.start()
        kept = pltpu.make_async_copy(own_ref.at[:, lanes(xl, 128)], do_ref.at[xl], sems.at[0, base + 1])
        kept.start()
        kept.wait()
        yield

        def block(query_half, key_half, qb, h, diagonal):
            qs = rows_of(qb)
            hs = slice(h * HEAD, (h + 1) * HEAD)
            do = do_ref[query_half, qs, :]
            qh = only(x_ref[query_half, qs, Q] * jnp.asarray(HEAD**-0.5, BF), h)
            doh = only(do, h)
            delta = jnp.sum(
                doh.astype(F32).T[hs] * ot_ref[query_half, hs, qs], axis=0, keepdims=True
            )
            lse = lse_ref[query_half, h : h + 1, qs]
            for kb in range(qb + 1 if diagonal else 2):
                ks = rows_of(kb)
                k = x_ref[key_half, ks, K]
                scores = dot_nt(k, qh)
                probs = jnp.exp(scores - lse)
                allowed = allowed_mask(first_len, key_half, kb, query_half, qb, diagonal)
                if allowed is not None:
                    probs = jnp.where(allowed, probs, 0.0)
                pulled = dot_nt(x_ref[key_half, ks, V], doh)
                ds = (probs * (pulled - delta)).astype(BF)
                dv = dot_nn(probs.astype(BF), doh)
                dk = dot_nn(ds, qh)
                dq = dot_tn(only(k, h), ds)[hs]
                if diagonal and h == 0 and qb == kb:
                    dv_ref[key_half, ks, :] = dv
                    dk_ref[key_half, ks, :] = dk
                else:
                    dv_ref[key_half, ks, :] += dv
                    dk_ref[key_half, ks, :] += dk
                if diagonal and kb == 0:
                    dqt_ref[query_half, hs, qs] = dq
                else:
                    dqt_ref[query_half, hs, qs] += dq

        def finish(half):
            for b in range(2):
                bs = rows_of(b)
                cosine, below, above = rotary_tables(angles_ref[half, :, bs])
                dq = dqt_ref[half, :, bs].T * HEAD**-0.5
                half_ref[half, bs, Q] = rotate(dq, cosine, -below, -above).astype(BF)
                half_ref[half, bs, K] = rotate(dk_ref[half, bs, :], cosine, -below, -above).astype(BF)
                half_ref[half, bs, V] = dv_ref[half, bs, :].astype(BF)

        for qb in range(2):
            for h in range(2):
                block(xl, xl, qb, h, True)
        yield
        sent.wait_recv()
        for qb in range(2):
            for h in range(2):
                block(1 - xl, 1 - xl, qb, h, True)
        yield
        for qb in range(2):
            for h in range(2):
                block(1, 0, qb, h, False)
            yield
        finish(1 - xl)
        back = remote(half_ref.at[1 - xl], out_ref.at[:, lanes(xl, 384)], sems, base + 2, pair)
        back.start()
        finish(xl)
        mine = pltpu.make_async_copy(half_ref.at[xl], out_ref.at[:, lanes(xl, 384)], sems.at[0, base + 3])
        mine.start()
        pending += [sent, back]
        yield
        mine.wait()
        back.wait_recv()


def feed_kernel(h_ref, dy_ref, gate_ref, up_ref, down_ref, hid_ref, dg_ref, du_ref, dh_ref):
    gate, up = dot_nn(h_ref[...], gate_ref[...]), dot_nn(h_ref[...], up_ref[...])
    sigmoid = jax.nn.sigmoid(gate)
    activated = gate * sigmoid
    hidden = (activated * up).astype(BF)
    hid_ref[...] = hidden
    d_hidden = dot_nt(dy_ref[...], down_ref[...])
    d_gate = (d_hidden * up * sigmoid * (1.0 + gate * (1.0 - sigmoid))).astype(BF)
    d_up = (d_hidden * activated).astype(BF)
    dg_ref[...] = d_gate
    du_ref[...] = d_up
    dh_ref[...] = (dot_nt(d_gate, gate_ref[...]) + dot_nt(d_up, up_ref[...])).astype(BF)


def feed_call(h, dy, w_gate, w_up, w_down):
    return pl.pallas_call(
        feed_kernel,
        out_shape=(
            jax.ShapeDtypeStruct((HALF, 768), BF),
            jax.ShapeDtypeStruct((HALF, 768), BF),
            jax.ShapeDtypeStruct((HALF, 768), BF),
            jax.ShapeDtypeStruct((HALF, D), BF),
        ),
        grid=(HALF // ROWS,),
        in_specs=[rowwise(D), rowwise(D), fixed(D, 768), fixed(D, 768), fixed(768, D)],
        out_specs=(rowwise(768), rowwise(768), rowwise(768), rowwise(D)),
        compiler_params=pltpu.CompilerParams(vmem_limit_bytes=34 << 20),
        cost_estimate=pl.CostEstimate(
            flops=5 * 2 * HALF * D * 768, bytes_accessed=26 << 20, transcendentals=HALF * 768
        ),
    )(h, dy, w_gate, w_up, w_down)


def wide_update_kernel(qkv_ref, gate_ref, up_ref, *refs):
    ins, outs = refs[:9], refs[9:]

    def update(k, at, gradient):
        new = adamw(*[ref[:, at] for ref in ins[k * 3 : k * 3 + 3]], gradient, D ** (-0.5), 0.1)
        for ref, value in zip(outs[k * 3 : k * 3 + 3], new):
            ref[:, at] = value

    for k in range(8):
        for pair in range(2):
            for kind in range(3):
                update(
                    0,
                    columns(kind * D + k * 256 + pair * 128, 128),
                    qkv_ref[k, :, columns(pair * 384 + kind * 128, 128)].astype(F32),
                )
    pieces = [(o * 44, o % 8, o // 8 * 48, 44) for o in range(128)]
    for w, grad_ref in enumerate((gate_ref, up_ref)):
        for tile in range(FF // 128):
            value = moved(lambda k, at: grad_ref[k, :, at], tile, pieces, 768 - 256)
            update(1 + w, columns(tile * 128, 128), value)


def wide_updates(grads, *states):
    operands = [x for state in states for x in state]
    return pl.pallas_call(
        wide_update_kernel,
        out_shape=[jax.ShapeDtypeStruct(x.shape, F32) for x in operands],
        in_specs=[pl.BlockSpec(memory_space=pltpu.VMEM)] * 12,
        out_specs=[pl.BlockSpec(memory_space=pltpu.VMEM)] * 9,
        compiler_params=pltpu.CompilerParams(vmem_limit_bytes=24 << 20),
        cost_estimate=pl.CostEstimate(flops=20 << 20, bytes_accessed=10 << 20, transcendentals=1 << 20),
    )(*grads, *operands)


TO_HEADS = [(f * 16 + ctx, ctx * 8 + f) for f in range(8) for ctx in range(16)]
TO_OWNER = [(b, a) for a, b in TO_HEADS]


def local(
    hidden_in, out_grad, positions, documents,
    qkv_weight, qkv_first, qkv_second,
    out_weight, out_first, out_second,
    gate_weight, gate_first, gate_second,
    up_weight, up_first, up_second,
    down_weight, down_first, down_second,
    small_params, small_first, small_second,
):
    xh, xl, z = lax.axis_index("xh"), lax.axis_index("xl"), lax.axis_index("z")
    yc = lax.axis_index("y") * 2 + lax.axis_index("core")
    place = (z * 2 + xh) * 2 + xl

    first_here = jnp.sum(1 - documents)
    start_here = positions[0, 0]
    marks = jnp.stack([first_here, start_here // 64, start_here % 64]).astype(BF)
    tile = jnp.concatenate(
        [small_params.astype(BF), jnp.pad(marks, (0, 13))[None]], axis=0
    )
    tile = jnp.where((jnp.arange(8) == yc)[None, :, None], tile[:, None, :], 0)
    tile = jnp.pad(tile.reshape(8, 128), ((0, 8), (0, 0)))
    outer = out_grad.reshape(128, D)
    out_rows = lax.ppermute(out_weight.astype(BF), AXES, TO_HEADS)
    share, units = ShareQkv(), GatherTokens(128, D, normalize=True, far=True)
    w_all, params, u_all, gu_mine, w_out, h1, qkv, angles = comm(
        0,
        "adbccdddccddabccdccaacaaabbabbaabce",
        (share, (qkv_weight, tile)),
        (units, (hidden_in,)),
        (ShareHidden(), (gate_weight, up_weight)),
        (GatherSmall(16, D), (out_rows,)),
        (MakeQkv(share, units), ()),
    )
    u_all, w_qkv, w_out = u_all.reshape(HALF, D), w_all.reshape(D, 896), w_out.reshape(256, D)
    gu_mine = gu_mine.reshape(128, 1536)
    o, attended_t, lse, heads, dy, w_gate = comm(
        1,
        "abcabbccacbbaaccabca",
        (Attend(), (params, qkv)),
        (GatherTokens(128, D, far=True), (outer,)),
        (GatherWeights(128, 768), (gu_mine[:, :768],)),
    )
    dy = dy.reshape(HALF, D)
    branch_part = dot_nn(o, w_out).astype(BF)
    branch, w_up = comm(
        2,
        "ababbbbaabbab",
        (SumTokens(128, D), (branch_part,)),
        (GatherWeights(128, 768), (gu_mine[:, 768:],)),
    )
    rows = hidden_in.reshape(128, D).astype(F32)
    middle = rows + branch
    normed_two, unit_two, scale_two = norm_forward(middle, params[5], params[6])
    down_piece = jnp.pad(down_weight.astype(BF), ((0, 4), (0, 0)))
    h2, w_down = comm(
        3,
        "abbbbaabbaabab",
        (GatherTokens(128, D), (normed_two.astype(BF),)),
        (GatherWeights(48, D), (down_piece,)),
    )
    h2 = h2.reshape(HALF, D)
    w_down = w_down.reshape(768, D)
    hidden, d_gate_low, d_up_low, dh2_part = feed_call(
        h2, dy, w_gate.reshape(D, 768), w_up.reshape(D, 768), w_down
    )

    d_normed_two, g_down, d_gate, d_up = comm(
        4,
        "abbbaccbbaacccbccbbacb",
        (SumTokens(128, D), (dh2_part,)),
        (GradThenSum(768, D, 2), (hidden, dy)),
        (TokenSums(D, 768, 2), (h2, d_gate_low, d_up_low)),
    )
    d_middle_part, d_gain_two, d_shift_two = norm_backward(
        d_normed_two, unit_two, scale_two, params[5]
    )
    d_middle = outer.astype(F32) + d_middle_part
    dx2, g_gate, y_part = comm(
        5,
        "abcbbcaacbbbcaaab",
        (GatherTokens(128, D), (d_middle.astype(BF),)),
        (SumWeights(128, 768), (d_gate,)),
        (Product(768, D), (hidden, w_down)),
    )
    dx2 = dx2.reshape(HALF, D)
    do = dot_nt(dx2, w_out).astype(BF)
    d_qkv_low, block_out, g_up, gate_back = comm(
        7,
        "abcdabaccaaabbcccdbca",
        (AttendBack(), (params, heads, do, attended_t, lse, angles)),
        (SumTokens(128, D, plus=True), (y_part, middle)),
        (SumFew(128, 768), (d_up,)),
        (Swap(16, 768), (g_gate,)),
    )
    d_out = dot_tn(o, dx2).astype(BF)
    zeros = jnp.zeros((5, D), F32)
    last = LastRows()
    input_grad, qkv_back, g_out, g_small, up_back = comm(
        6,
        "ecbbbbbaaccaadbbacdbaaccdddbbcddabdb",
        (last, (d_qkv_low, u_all, w_qkv, hidden_in, d_middle, params)),
        (GradThenSum(D, 768, 4, swap=True), (h1, d_qkv_low)),
        (SumFew(16, D), (d_out,)),
        (SumSmall(last), (jnp.concatenate([zeros, d_gain_two[None], d_shift_two[None], zeros[:1]]),)),
        (Swap(16, 768), (g_up,)),
    )
    block_out, input_grad = block_out.reshape(1, 128, D), input_grad.reshape(1, 128, D)

    small = lax.dynamic_slice_in_dim(g_small, place * 16, 16, axis=1)
    owned = lax.ppermute(
        jnp.concatenate([g_out, jnp.pad(small, ((0, 0), (0, 112)))], axis=1), AXES, TO_OWNER
    )
    g_out, g_small = owned[:, :D].astype(F32), owned[:7, D : D + 16].astype(F32)

    wide = wide_updates(
        (qkv_back, gate_back, up_back),
        (qkv_weight, qkv_first, qkv_second),
        (gate_weight, gate_first, gate_second),
        (up_weight, up_first, up_second),
    )
    updates = (
        wide[0:3],
        adamw(out_weight, out_first, out_second, g_out, (D // 16) ** (-0.5), 0.1),
        wide[3:6],
        wide[6:9],
        adamw(down_weight, down_first, down_second, g_down[:44].astype(F32), FF ** (-0.5), 0.1),
        adamw(small_params, small_first, small_second, g_small, 2.0, 0.0),
    )
    return (block_out, input_grad, *[x for u in updates for x in u])


def solution(mesh):
    fine = Mesh(mesh.devices.reshape(4, 2, 2, 4, 2), AXES)
    tokens = P(("z", "xh"), ("xl", "y", "core"), None)
    marks = P(("z", "xh"), ("xl", "y", "core"))
    rows = P(AXES, None)
    small = P(None, AXES)
    in_specs = (tokens, tokens, marks, marks) + (rows,) * 15 + (small,) * 3
    out_specs = (tokens, tokens) + (rows,) * 15 + (small,) * 3
    return jax.shard_map(local, mesh=fine, in_specs=in_specs, out_specs=out_specs, check_vma=False)
```

profile of v0, /device:TPU:25, one launch (start us, length us, event | category | flops | bytes accessed | tf_op | source)
XLA Modules:
  0.0 360.4 jit_solution(15009878116629960273)
XLA Ops:
  0.7 0.9 convert_element_type.51
  1.6 5.9 %collective-permute-start = (bf16[16,2048]{1,0:T(8,128)(2,1)S(1)}, bf16[16,2048]{1,0:T(8,128)(2,1)S(1)}, u32[]{:S(2)}, u32[]{:S(2)}) collective-permute-start(bf16[16,2048]{1,0:T(8,128)(2,1)S(1)} %convert_element_type.51), channel_id=1, source_target_pairs={{0,0},{1,8},{2,16},{3,24},{4,32},{5,40},{6,48},{7,56},{8,64},{9,72... | collective-permute-start | bytes 196616 | tf_op jit(solution)/shard_map/ppermute | solution.py:1408
  10.1 1.3 subtract_reduce_fusion
  12.1 0.7 convert_element_type.50
  12.8 0.1 fusion.8
  12.9 0.1 broadcast_in_dim.49
  13.0 0.1 broadcast_in_dim.44
  13.1 0.1 broadcast_in_dim.45
  13.2 1.0 convert_element_type.56
  14.2 0.1 pad.25.clone
  14.3 0.0 collective-permute-done.refs_5_
  14.3 45.0 %shard_map.365 = (bf16[4,4,128,896]{3,2,1,0:T(8,128)(2,1)}, f32[16,2048]{1,0:T(8,128)S(1)}, bf16[8,128,2048]{2,1,0:T(8,128)(2,1)}, bf16[8,16,1536]{2,1,0:T(8,128...) custom-call(f32[16,6144]{1,0:T(8,128)} %refs_0_.3, ...), custom_call_target="tpu_custom_call" | custom-call | bytes 305397760 | tf_op jit(solution)/shard_map/pallas_call | solution.py:1011
  59.4 2.0 copy-done.1
  61.5 46.4 %shard_map.366 = (bf16[1024,256]{1,0:T(8,128)(2,1)S(1)}, f32[2,128,1024]{2,1,0:T(8,128)S(1)}, f32[2,8,1024]{2,1,0:T(8,128)S(1)}, bf16[2,1024,384]{2,1,0:T(8,128)...) custom-call(f32[16,2048]{1,0:T(8,128)S(1)} %get-tuple-element.67.refs_0_.refs_5_, ...), custom_call_target="tpu_custom_call" | custom-call | bytes 199884800 | tf_op jit(solution)/shard_map/pallas_call | solution.py:1011
  107.9 1.0 copy-done.8
  108.8 1.8 convolution_convert_fusion
  110.6 0.0 copy-start
  110.6 23.9 %shard_map.367 = (f32[128,2048]{1,0:T(8,128)S(1)}, bf16[4,4,128,768]{3,2,1,0:T(8,128)(2,1)S(1)}) custom-call(bf16[8,128,2048]{2,1,0:T(8,128)(2,1)S(1)} %bitcast.44, bf16[128,768]{1,0:T(8,128)(2,1)S(1)} %get-tuple-element.131.refs_1_), custom_call_target="tpu_custom_call" | custom-call | bytes 73400320 | tf_op jit(solution)/shard_map/pallas_call | solution.py:1011
  134.6 0.2 fusion.16
  134.8 0.3 multiply_reduce_fusion.2
  135.0 0.3 add_convert_fusion.refs_0_
  135.3 23.8 %shard_map.368 = (bf16[8,128,2048]{2,1,0:T(8,128)(2,1)S(1)}, bf16[4,4,48,2048]{3,2,1,0:T(8,128)(2,1)S(1)}) custom-call(bf16[128,2048]{1,0:T(8,128)(2,1)S(1)} %add_convert_fusion.refs_0_, bf16[48,2048]{1,0:T(8,128)(2,1)S(1)} %pad.18.refs_1_), custom_call_target="tpu_custom_call" | custom-call | bytes 146800640 | tf_op jit(solution)/shard_map/pallas_call | solution.py:1011
  159.1 1.9 copy-done.2
  161.0 21.9 %shard_map.369 = (bf16[1024,768]{1,0:T(8,128)(2,1)S(1)}, bf16[1024,768]{1,0:T(8,128)(2,1)S(1)}, bf16[1024,768]{1,0:T(8,128)(2,1)S(1)}, bf16[1024,2048]{1,0:T(8,128)(2,1)S(1)}) custom-call(bf16[1024,2048]{1,0:T(8,128)(2,1)} %bitcast.48, bf16[1024,2048]{1,0:T(8,128)(2,1)} %bitcast.68, bf16[2048,768]{1,0:T(8,128)(2,1)S(1)} %bitcast.65, ...), custom_call_target="tpu_custom_call" | custom-call | flops 16106127360 | bytes 27262976 | tf_op jit(solution)/shard_map/pallas_call | solution.py:1329
  182.9 1.9 copy-done.3
  184.8 33.9 %shard_map.370 = (f32[128,2048]{1,0:T(8,128)S(1)}, bf16[48,2048]{1,0:T(8,128)(2,1)S(1)}, bf16[2048,768]{1,0:T(8,128)(2,1)S(1)}, bf16[2048,768]{1,0:T(8,128)(2,1)}) custom-call(bf16[8,128,2048]{2,1,0:T(8,128)(2,1)} %bitcast.50, bf16[1024,768]{1,0:T(8,128)(2,1)S(1)} %get-tuple-element.80.refs_1_.refs_2_, bf16[1024,2048]{1,0:T(8,128)(2,1)} %bitcast.69, ...), custom_call_target="tpu_custom_call" | custom-call | bytes 140247040 | tf_op jit(solution)/shard_map/pallas_call | solution.py:1011
  218.8 0.4 multiply_reduce_fusion
  219.2 0.7 fusion.15
  219.9 27.0 %shard_map.371 = (bf16[8,128,2048]{2,1,0:T(8,128)(2,1)S(1)}, bf16[128,768]{1,0:T(8,128)(2,1)S(1)}, bf16[1024,2048]{1,0:T(8,128)(2,1)S(1)}) custom-call(bf16[128,2048]{1,0:T(8,128)(2,1)S(1)} %get-tuple-element.127.refs_0_, bf16[4,4,128,768]{3,2,1,0:T(8,128)(2,1)S(1)} %bitcast.54, bf16[1024,768]{1,0:T(8,128)(2,1)S(1)} %get-tuple-element.80.refs_1_.refs_2_, ...), custom_call_target="tpu_custom_call" | custom-call | bytes 171704320 | tf_op jit(solution)/shard_map/pallas_call | solution.py:1011
  246.9 0.0 copy-start.11
  246.9 1.3 convolution_convert_fusion.1
  248.2 1.3 convolution_convert_fusion.2.refs_2_
  249.5 0.1 maximum_maximum_fusion.refs_9_
  249.6 0.5 copy-done.4
  250.1 0.3 copy-done.9
  250.4 45.1 %shard_map.372 = (bf16[1024,768]{1,0:T(8,128)(2,1)S(1)}, bf16[128,2048]{1,0:T(8,128)(2,1)S(1)}, bf16[128,768]{1,0:T(8,128)(2,1)S(1)}, bf16[8,16,768]{2,1,0:T(8,128)(2,1)S(1)}) custom-call(f32[16,2048]{1,0:T(8,128)S(1)} %get-tuple-element.67.refs_0_.refs_5_, bf16[2,1024,384]{2,1,0:T(8,128)(2,1)S(1)} %get-tuple-element.70.refs_1_, ...), custom_call_target="tpu_custom_call" | custom-call | bytes 49807360 | tf_op jit(solution)/shard_map/pallas_call | solution.py:1011
  295.5 0.0 copy-start.19
  295.5 0.0 copy-start.21
  295.6 0.0 copy-start.22
  295.6 0.0 copy-start.5
  295.6 0.0 copy-start.6
  295.6 0.0 copy-start.7
  295.6 0.0 copy-start.12
  295.6 0.0 copy-start.13
  295.6 0.0 copy-start.14
  295.6 0.0 copy-start.15
  295.7 0.0 copy-start.16
  295.7 0.0 copy-start.17
  295.7 49.7 %shard_map.373 = (f32[128,2048]{1,0:T(8,128)S(1)}, bf16[8,16,768]{2,1,0:T(8,128)(2,1)S(1)}, bf16[16,2048]{1,0:T(8,128)(2,1)S(1)}, bf16[16,512]{1,0:T(8,128)(2,1)S(1)}, bf16[8,16,768]{2,1,0:T(8,128)(2,1)S(1)}) custom-call(bf16[1024,768]{1,0:T(8,128)(2,1)S(1)} %get-tuple-element.93.refs_0_.refs_7_, bf16[1024,2048]{1,0:T(8,128)(2,1)} %bitcast.67, ...), custom_call_target="tpu_custom_call" | custom-call | bytes 19988480 | tf_op jit(solution)/shard_map/pallas_call | solution.py:1011
  345.3 0.0 copy-start.20
  345.4 0.0 copy-start.23
  345.4 0.0 copy-start.24
  345.4 0.0 copy-start.25
  345.4 0.0 copy-start.26
  345.4 0.0 copy-start.27
  345.4 0.1 constant_dynamic-slice_fusion
  345.5 5.2 %collective-permute-start.1 = (bf16[16,2176]{1,0:T(8,128)(2,1)S(1)}, bf16[16,2176]{1,0:T(8,128)(2,1)S(1)}, u32[]{:S(2)}, u32[]{:S(2)}) collective-permute-start(bf16[16,2176]{1,0:T(8,128)(2,1)S(1)} %fusion.5), channel_id=1, source_target_pairs={{0,0},{8,1},{16,2},{24,3},{32,4},{40,5},{48,6},{56,7},{64,8},{72,9... | collective-permute-start | bytes 208904 | tf_op jit(solution)/shard_map/ppermute | solution.py:1495
  350.7 1.2 multiply_subtract_fusion
  352.0 2.8 shard_map.374
  354.8 2.2 collective-permute-done.1
  357.0 0.8 multiply_subtract_fusion.1
  357.8 0.6 multiply_subtract_fusion.2
  358.4 0.8 copy.44
  359.2 1.0 copy.45
  (44 shorter events, 0.2 us)
Async XLA Ops:
  1.6 12.8 %collective-permute-start = (bf16[16,2048]{1,0:T(8,128)(2,1)S(1)}, bf16[16,2048]{1,0:T(8,128)(2,1)S(1)}, u32[]{:S(2)}, u32[]{:S(2)}) collective-permute-start(bf16[16,2048]{1,0:T(8,128)(2,1)S(1)} %convert_element_type.51), channel_id=1, source_target_pairs={{0,0},{1,8},{2,16},{3,24},{4,32},{5,40},{6,48},{7,56},{8,64},{9,72... | collective-permute-start | bytes 196616 | tf_op jit(solution)/shard_map/ppermute | solution.py:1408
  59.4 2.0 copy-start.1
  61.4 49.2 %copy-start.10 = (bf16[4,4,16,2048]{3,2,1,0:T(8,128)(2,1)}, bf16[4,4,16,2048]{3,2,1,0:T(8,128)(2,1)S(1)}, u32[]{:S(2)}) copy-start(bf16[4,4,16,2048]{3,2,1,0:T(8,128)(2,1)S(1)} %get-tuple-element.72) | copy-start | bytes 3145732
  107.9 1.0 copy-start.8
  110.6 23.9 %copy-start = (bf16[1,128,2048]{2,1,0:T(8,128)(2,1)S(1)}, bf16[1,128,2048]{2,1,0:T(8,128)(2,1)}, u32[]{:S(2)}) copy-start(bf16[1,128,2048]{2,1,0:T(8,128)(2,1)} %param.22) | copy-start | bytes 1572868
  159.1 1.9 copy-start.2
  182.9 1.9 copy-start.3
  184.8 34.4 %copy-start.18 = (bf16[1,128,2048]{2,1,0:T(8,128)(2,1)S(1)}, bf16[1,128,2048]{2,1,0:T(8,128)(2,1)}, u32[]{:S(2)}) copy-start(bf16[1,128,2048]{2,1,0:T(8,128)(2,1)} %param.23) | copy-start | bytes 1572868
  246.9 1.3 copy-start.11
  248.2 1.9 copy-start.4
  248.2 2.2 copy-start.9
  295.5 55.2 %copy-start.19 = (f32[44,2048]{1,0:T(8,128)S(1)}, f32[44,2048]{1,0:T(8,128)}, u32[]{:S(2)}) copy-start(f32[44,2048]{1,0:T(8,128)} %param.38) | copy-start | bytes 1081348
  295.5 55.2 %copy-start.21 = (f32[44,2048]{1,0:T(8,128)S(1)}, f32[44,2048]{1,0:T(8,128)}, u32[]{:S(2)}) copy-start(f32[44,2048]{1,0:T(8,128)} %param.39) | copy-start | bytes 1081348
  295.6 55.2 %copy-start.22 = (f32[44,2048]{1,0:T(8,128)S(1)}, f32[44,2048]{1,0:T(8,128)}, u32[]{:S(2)}) copy-start(f32[44,2048]{1,0:T(8,128)} %param.40) | copy-start | bytes 1081348
  295.6 56.4 %copy-start.5 = (f32[16,6144]{1,0:T(8,128)S(1)}, f32[16,6144]{1,0:T(8,128)}, u32[]{:S(2)}) copy-start(f32[16,6144]{1,0:T(8,128)} %refs_0_.3) | copy-start | bytes 1179652
  295.6 56.4 %copy-start.6 = (f32[16,5632]{1,0:T(8,128)S(1)}, f32[16,5632]{1,0:T(8,128)}, u32[]{:S(2)}) copy-start(f32[16,5632]{1,0:T(8,128)} %refs_3_.3) | copy-start | bytes 1081348
  295.6 56.3 %copy-start.7 = (f32[16,5632]{1,0:T(8,128)S(1)}, f32[16,5632]{1,0:T(8,128)}, u32[]{:S(2)}) copy-start(f32[16,5632]{1,0:T(8,128)} %refs_6_.1) | copy-start | bytes 1081348
  295.6 56.3 %copy-start.12 = (f32[16,6144]{1,0:T(8,128)S(1)}, f32[16,6144]{1,0:T(8,128)}, u32[]{:S(2)}) copy-start(f32[16,6144]{1,0:T(8,128)} %refs_1_.1) | copy-start | bytes 1179652
  295.6 56.3 %copy-start.13 = (f32[16,6144]{1,0:T(8,128)S(1)}, f32[16,6144]{1,0:T(8,128)}, u32[]{:S(2)}) copy-start(f32[16,6144]{1,0:T(8,128)} %refs_2_.1) | copy-start | bytes 1179652
  295.6 56.3 %copy-start.14 = (f32[16,5632]{1,0:T(8,128)S(1)}, f32[16,5632]{1,0:T(8,128)}, u32[]{:S(2)}) copy-start(f32[16,5632]{1,0:T(8,128)} %refs_4_.3) | copy-start | bytes 1081348
  295.6 56.3 %copy-start.15 = (f32[16,5632]{1,0:T(8,128)S(1)}, f32[16,5632]{1,0:T(8,128)}, u32[]{:S(2)}) copy-start(f32[16,5632]{1,0:T(8,128)} %refs_5_.1) | copy-start | bytes 1081348
  295.7 56.3 %copy-start.16 = (f32[16,5632]{1,0:T(8,128)S(1)}, f32[16,5632]{1,0:T(8,128)}, u32[]{:S(2)}) copy-start(f32[16,5632]{1,0:T(8,128)} %refs_7_.1) | copy-start | bytes 1081348
  295.7 56.3 %copy-start.17 = (f32[16,5632]{1,0:T(8,128)S(1)}, f32[16,5632]{1,0:T(8,128)}, u32[]{:S(2)}) copy-start(f32[16,5632]{1,0:T(8,128)} %refs_8_.1) | copy-start | bytes 1081348
  345.3 11.6 %copy-start.20 = (f32[16,2048]{1,0:T(8,128)S(1)}, f32[16,2048]{1,0:T(8,128)}, u32[]{:S(2)}) copy-start(f32[16,2048]{1,0:T(8,128)} %param.29) | copy-start | bytes 393220
  345.4 11.6 %copy-start.23 = (f32[16,2048]{1,0:T(8,128)S(1)}, f32[16,2048]{1,0:T(8,128)}, u32[]{:S(2)}) copy-start(f32[16,2048]{1,0:T(8,128)} %param.30) | copy-start | bytes 393220
  345.4 11.6 %copy-start.24 = (f32[16,2048]{1,0:T(8,128)S(1)}, f32[16,2048]{1,0:T(8,128)}, u32[]{:S(2)}) copy-start(f32[16,2048]{1,0:T(8,128)} %param.31) | copy-start | bytes 393220
  345.4 12.4 %copy-start.25 = (f32[7,16]{1,0:T(8,128)S(1)}, f32[7,16]{1,0:T(8,128)}, u32[]{:S(2)}) copy-start(f32[7,16]{1,0:T(8,128)} %param.41) | copy-start | bytes 1348
  345.4 12.4 %copy-start.26 = (f32[7,16]{1,0:T(8,128)S(1)}, f32[7,16]{1,0:T(8,128)}, u32[]{:S(2)}) copy-start(f32[7,16]{1,0:T(8,128)} %param.42) | copy-start | bytes 1348
  345.4 12.4 %copy-start.27 = (f32[7,16]{1,0:T(8,128)S(1)}, f32[7,16]{1,0:T(8,128)}, u32[]{:S(2)}) copy-start(f32[7,16]{1,0:T(8,128)} %param.43) | copy-start | bytes 1348
  345.5 11.5 %collective-permute-start.1 = (bf16[16,2176]{1,0:T(8,128)(2,1)S(1)}, bf16[16,2176]{1,0:T(8,128)(2,1)S(1)}, u32[]{:S(2)}, u32[]{:S(2)}) collective-permute-start(bf16[16,2176]{1,0:T(8,128)(2,1)S(1)} %fusion.5), channel_id=1, source_target_pairs={{0,0},{8,1},{16,2},{24,3},{32,4},{40,5},{48,6},{56,7},{64,8},{72,9... | collective-permute-start | bytes 208904 | tf_op jit(solution)/shard_map/ppermute | solution.py:1495
where the time goes:
time: 366 us; the launch traced here: 360 us
  Pallas kernels  320 us (87%)
  starting transfers between devices  11.1 us (3%)
  local copies, waits for them, and re-layouts  10 us (3%)
  other arithmetic  8.56 us (2%)
  between operations  4.67 us (1%)
  matrix products  4.34 us (1%)
    pallas_call x8, Pallas kernels, comm(): pl.pallas_call(functools.partial(comm_kernel, parts, order), out_shape=[(...  295 us
    pallas_call x1, Pallas kernels, feed_call(): pl.pallas_call(feed_kernel, out_shape=(jax.ShapeDtypeStruct((HALF, 768),...  21.9 us
    unnamed x58, local copies, waits for them, and re-layouts  9.52 us
  transfers between devices with their start and end apart: 2, of which 1 were waited for; matrix products, arithmetic and copies ran while one was open for 1% of the time, Pallas kernels for 1%

commit v1 on v0

--- a/solution.py
+++ b/solution.py
@@ -937,6 +937,11 @@
 
 def size(shape, dtype):
     return math.prod(shape) * jnp.dtype(dtype).itemsize
+
+
+def far(part, *which):
+    part.ins = [(*spec[:2], "far") if k in which else spec for k, spec in enumerate(part.ins)]
+    return part
 
 
 def loaded(part, copies):
@@ -1332,7 +1337,7 @@
             jax.ShapeDtypeStruct((HALF, 768), BF),
             jax.ShapeDtypeStruct((HALF, 768), BF),
             jax.ShapeDtypeStruct((HALF, 768), BF),
-            jax.ShapeDtypeStruct((HALF, D), BF),
+            pltpu.HBM((HALF, D), BF),
         ),
         grid=(HALF // ROWS,),
         in_specs=[rowwise(D), rowwise(D), fixed(D, 768), fixed(D, 768), fixed(768, D)],
@@ -1452,9 +1457,9 @@
     d_normed_two, g_down, d_gate, d_up = comm(
         4,
         "abbbaccbbaacccbccbbacb",
-        (SumTokens(128, D), (dh2_part,)),
-        (GradThenSum(768, D, 2), (hidden, dy)),
-        (TokenSums(D, 768, 2), (h2, d_gate_low, d_up_low)),
+        (far(SumTokens(128, D), 0), (dh2_part,)),
+        (far(GradThenSum(768, D, 2), 1), (hidden, dy)),
+        (far(TokenSums(D, 768, 2), 0), (h2, d_gate_low, d_up_low)),
     )
     d_middle_part, d_gain_two, d_shift_two = norm_backward(
         d_normed_two, unit_two, scale_two, params[5]
@@ -1483,8 +1488,8 @@
     input_grad, qkv_back, g_out, g_small, up_back = comm(
         6,
         "ecbbbbbaaccaadbbacdbaaccdddbbcddabdb",
-        (last, (d_qkv_low, u_all, w_qkv, hidden_in, d_middle, params)),
-        (GradThenSum(D, 768, 4, swap=True), (h1, d_qkv_low)),
+        (far(last, 1, 2), (d_qkv_low, u_all, w_qkv, hidden_in, d_middle, params)),
+        (far(GradThenSum(D, 768, 4, swap=True), 0), (h1, d_qkv_low)),
         (SumFew(16, D), (d_out,)),
         (SumSmall(last), (jnp.concatenate([zeros, d_gain_two[None], d_shift_two[None], zeros[:1]]),)),
         (Swap(16, 768), (g_up,)),

time: 366 us -> 360 us (0.984)
  Pallas kernels: 320 us -> 314 us
    pallas_call x8, Pallas kernels: 295 us -> 288 us  [comm(): pl.pallas_call(functools.partial(comm_kernel, parts, order), out_shape=[(...]
    unnamed x58 -> x64, local copies, waits for them, and re-layouts: 9.52 us -> 8.13 us
where the time goes in v1:
time: 360 us; the launch traced here: 354 us
  Pallas kernels  314 us (87%)
  starting transfers between devices  11.8 us (3%)
  local copies, waits for them, and re-layouts  8.62 us (2%)
  other arithmetic  8.57 us (2%)
  between operations  4.7 us (1%)
  matrix products  4.33 us (1%)
    pallas_call x8, Pallas kernels, comm(): pl.pallas_call(functools.partial(comm_kernel, parts, order), out_shape=[(...  288 us
    pallas_call x1, Pallas kernels, feed_call(): pl.pallas_call(feed_kernel, out_shape=(jax.ShapeDtypeStruct((HALF, 768),...  23.7 us
    unnamed x64, local copies, waits for them, and re-layouts  8.13 us
  transfers between devices with their start and end apart: 2, of which 1 were waited for; matrix products, arithmetic and copies ran while one was open for 1% of the time, Pallas kernels for 1%

profile of v1, /device:TPU:25, one launch (start us, length us, event | category | flops | bytes accessed | tf_op | source)
XLA Modules:
  0.0 353.8 jit_solution(6767460290722360358)
XLA Ops:
  0.7 0.9 convert_element_type.51
  1.6 5.9 %collective-permute-start = (bf16[16,2048]{1,0:T(8,128)(2,1)S(1)}, bf16[16,2048]{1,0:T(8,128)(2,1)S(1)}, u32[]{:S(2)}, u32[]{:S(2)}) collective-permute-start(bf16[16,2048]{1,0:T(8,128)(2,1)S(1)} %convert_element_type.51), channel_id=1, source_target_pairs={{0,0},{1,8},{2,16},{3,24},{4,32},{5,40},{6,48},{7,56},{8,64},{9,72... | collective-permute-start | bytes 196616 | tf_op jit(solution)/shard_map/ppermute | solution.py:1413
  10.1 1.3 subtract_reduce_fusion
  12.1 0.7 convert_element_type.50
  12.8 0.1 fusion.8
  12.9 0.1 broadcast_in_dim.49
  13.0 0.1 broadcast_in_dim.44
  13.1 0.1 broadcast_in_dim.45
  13.2 1.0 convert_element_type.56
  14.2 0.1 pad.25.clone
  14.3 45.0 %shard_map.365 = (bf16[4,4,128,896]{3,2,1,0:T(8,128)(2,1)}, f32[16,2048]{1,0:T(8,128)S(1)}, bf16[8,128,2048]{2,1,0:T(8,128)(2,1)}, bf16[8,16,1536]{2,1,0:T(8,128...) custom-call(f32[16,6144]{1,0:T(8,128)} %refs_0_.3, ...), custom_call_target="tpu_custom_call" | custom-call | bytes 305397760 | tf_op jit(solution)/shard_map/pallas_call | solution.py:1016
  59.4 2.0 copy-done.1
  61.4 46.4 %shard_map.366 = (bf16[1024,256]{1,0:T(8,128)(2,1)S(1)}, f32[2,128,1024]{2,1,0:T(8,128)S(1)}, f32[2,8,1024]{2,1,0:T(8,128)S(1)}, bf16[2,1024,384]{2,1,0:T(8,128)...) custom-call(f32[16,2048]{1,0:T(8,128)S(1)} %get-tuple-element.67.refs_0_.refs_5_, ...), custom_call_target="tpu_custom_call" | custom-call | bytes 199884800 | tf_op jit(solution)/shard_map/pallas_call | solution.py:1016
  107.8 1.2 copy-done.4
  109.0 1.0 copy-done.11
  110.0 0.8 copy-done.9
  110.8 1.8 convolution_convert_fusion
  112.6 0.0 copy-start
  112.6 23.9 %shard_map.367 = (f32[128,2048]{1,0:T(8,128)S(1)}, bf16[4,4,128,768]{3,2,1,0:T(8,128)(2,1)S(1)}) custom-call(bf16[8,128,2048]{2,1,0:T(8,128)(2,1)S(1)} %bitcast.44, bf16[128,768]{1,0:T(8,128)(2,1)S(1)} %get-tuple-element.131.refs_1_), custom_call_target="tpu_custom_call" | custom-call | bytes 73400320 | tf_op jit(solution)/shard_map/pallas_call | solution.py:1016
  136.5 0.2 fusion.16
  136.7 0.3 multiply_reduce_fusion.2
  137.0 0.3 add_convert_fusion.refs_0_
  137.3 23.8 %shard_map.368 = (bf16[8,128,2048]{2,1,0:T(8,128)(2,1)S(1)}, bf16[4,4,48,2048]{3,2,1,0:T(8,128)(2,1)S(1)}) custom-call(bf16[128,2048]{1,0:T(8,128)(2,1)S(1)} %add_convert_fusion.refs_0_, bf16[48,2048]{1,0:T(8,128)(2,1)S(1)} %pad.18.refs_1_), custom_call_target="tpu_custom_call" | custom-call | bytes 146800640 | tf_op jit(solution)/shard_map/pallas_call | solution.py:1016
  161.1 23.7 %shard_map.369 = (bf16[1024,768]{1,0:T(8,128)(2,1)S(1)}, bf16[1024,768]{1,0:T(8,128)(2,1)S(1)}, bf16[1024,768]{1,0:T(8,128)(2,1)S(1)}, bf16[1024,2048]{1,0:T(8,128)(2,1)}) custom-call(bf16[1024,2048]{1,0:T(8,128)(2,1)S(1)} %bitcast.48, bf16[1024,2048]{1,0:T(8,128)(2,1)} %bitcast.67, bf16[2048,768]{1,0:T(8,128)(2,1)S(1)} %bitcast.64, ...), custom_call_target="tpu_custom_call" | custom-call | flops 16106127360 | bytes 27262976 | tf_op jit(solution)/shard_map/pallas_call | solution.py:1334
  184.8 0.0 copy-start.21
  184.8 29.0 %shard_map.370 = (f32[128,2048]{1,0:T(8,128)S(1)}, bf16[48,2048]{1,0:T(8,128)(2,1)S(1)}, bf16[2048,768]{1,0:T(8,128)(2,1)S(1)}, bf16[2048,768]{1,0:T(8,128)(2,1)}) custom-call(bf16[8,128,2048]{2,1,0:T(8,128)(2,1)} %bitcast.69, bf16[1024,768]{1,0:T(8,128)(2,1)S(1)} %get-tuple-element.80.refs_1_.refs_2_, bf16[1024,2048]{1,0:T(8,128)(2,1)} %bitcast.68, ...), custom_call_target="tpu_custom_call" | custom-call | bytes 140247040 | tf_op jit(solution)/shard_map/pallas_call | solution.py:1016
  213.9 0.4 multiply_reduce_fusion
  214.3 0.7 fusion.15
  215.0 0.0 copy-start.10
  215.0 28.8 %shard_map.371 = (bf16[8,128,2048]{2,1,0:T(8,128)(2,1)S(1)}, bf16[128,768]{1,0:T(8,128)(2,1)S(1)}, bf16[1024,2048]{1,0:T(8,128)(2,1)S(1)}) custom-call(bf16[128,2048]{1,0:T(8,128)(2,1)S(1)} %get-tuple-element.127.refs_0_, bf16[4,4,128,768]{3,2,1,0:T(8,128)(2,1)S(1)} %bitcast.53, bf16[1024,768]{1,0:T(8,128)(2,1)S(1)} %get-tuple-element.80.refs_1_.refs_2_, ...), custom_call_target="tpu_custom_call" | custom-call | bytes 171704320 | tf_op jit(solution)/shard_map/pallas_call | solution.py:1016
  243.7 0.0 copy-start.14
  243.8 1.3 convolution_convert_fusion.1
  245.1 1.3 convolution_convert_fusion.2.refs_2_
  246.4 0.1 maximum_maximum_fusion.refs_9_
  246.5 0.5 copy-done.3
  246.9 0.5 copy-done.5
  247.4 0.3 copy-done.12
  247.7 43.2 %shard_map.372 = (bf16[1024,768]{1,0:T(8,128)(2,1)S(1)}, bf16[128,2048]{1,0:T(8,128)(2,1)S(1)}, bf16[128,768]{1,0:T(8,128)(2,1)S(1)}, bf16[8,16,768]{2,1,0:T(8,128)(2,1)S(1)}) custom-call(f32[16,2048]{1,0:T(8,128)S(1)} %get-tuple-element.67.refs_0_.refs_5_, bf16[2,1024,384]{2,1,0:T(8,128)(2,1)S(1)} %copy-done.5, ...), custom_call_target="tpu_custom_call" | custom-call | bytes 49807360 | tf_op jit(solution)/shard_map/pallas_call | solution.py:1016
  290.9 0.0 copy-start.22
  290.9 0.0 copy-start.24
  290.9 0.0 copy-start.25
  290.9 0.0 copy-start.6
  290.9 0.0 copy-start.7
  290.9 0.0 copy-start.8
  290.9 0.0 copy-start.15
  290.9 0.0 copy-start.16
  291.0 0.0 copy-start.17
  291.0 0.0 copy-start.18
  291.0 0.0 copy-start.19
  291.0 0.0 copy-start.20
  291.0 47.5 %shard_map.373 = (f32[128,2048]{1,0:T(8,128)S(1)}, bf16[8,16,768]{2,1,0:T(8,128)(2,1)S(1)}, bf16[16,2048]{1,0:T(8,128)(2,1)S(1)}, bf16[16,512]{1,0:T(8,128)(2,1)S(1)}, bf16[8,16,768]{2,1,0:T(8,128)(2,1)S(1)}) custom-call(bf16[1024,768]{1,0:T(8,128)(2,1)S(1)} %get-tuple-element.93.refs_0_.refs_7_, bf16[1024,2048]{1,0:T(8,128)(2,1)} %bitcast.66, ...), custom_call_target="tpu_custom_call" | custom-call | bytes 19988480 | tf_op jit(solution)/shard_map/pallas_call | solution.py:1016
  338.5 0.0 copy-start.23
  338.5 0.0 copy-start.26
  338.5 0.0 copy-start.29
  338.6 0.0 copy-start.30
  338.6 0.1 constant_dynamic-slice_fusion
  338.7 5.9 %collective-permute-start.1 = (bf16[16,2176]{1,0:T(8,128)(2,1)S(1)}, bf16[16,2176]{1,0:T(8,128)(2,1)S(1)}, u32[]{:S(2)}, u32[]{:S(2)}) collective-permute-start(bf16[16,2176]{1,0:T(8,128)(2,1)S(1)} %fusion.5), channel_id=1, source_target_pairs={{0,0},{8,1},{16,2},{24,3},{32,4},{40,5},{48,6},{56,7},{64,8},{72,9... | collective-permute-start | bytes 208904 | tf_op jit(solution)/shard_map/ppermute | solution.py:1500
  344.6 1.2 multiply_subtract_fusion
  345.8 2.8 shard_map.374
  348.7 1.7 collective-permute-done.1
  350.4 0.8 multiply_subtract_fusion.1
  351.2 0.6 multiply_subtract_fusion.2
  351.8 0.8 copy.44
  352.6 1.0 copy.45
  (50 shorter events, 0.2 us)
Async XLA Ops:
  1.6 12.8 %collective-permute-start = (bf16[16,2048]{1,0:T(8,128)(2,1)S(1)}, bf16[16,2048]{1,0:T(8,128)(2,1)S(1)}, u32[]{:S(2)}, u32[]{:S(2)}) collective-permute-start(bf16[16,2048]{1,0:T(8,128)(2,1)S(1)} %convert_element_type.51), channel_id=1, source_target_pairs={{0,0},{1,8},{2,16},{3,24},{4,32},{5,40},{6,48},{7,56},{8,64},{9,72... | collective-permute-start | bytes 196616 | tf_op jit(solution)/shard_map/ppermute | solution.py:1413
  59.4 2.0 copy-start.1
  61.4 51.2 %copy-start.13 = (bf16[4,4,16,2048]{3,2,1,0:T(8,128)(2,1)}, bf16[4,4,16,2048]{3,2,1,0:T(8,128)(2,1)S(1)}, u32[]{:S(2)}) copy-start(bf16[4,4,16,2048]{3,2,1,0:T(8,128)(2,1)S(1)} %get-tuple-element.72) | copy-start | bytes 3145732
  107.8 1.2 copy-start.4
  109.0 1.0 copy-start.11
  110.0 0.8 copy-start.9
  112.6 23.9 %copy-start = (bf16[1,128,2048]{2,1,0:T(8,128)(2,1)S(1)}, bf16[1,128,2048]{2,1,0:T(8,128)(2,1)}, u32[]{:S(2)}) copy-start(bf16[1,128,2048]{2,1,0:T(8,128)(2,1)} %param.22) | copy-start | bytes 1572868
  161.1 23.7 %copy-start.2 = (bf16[8,128,2048]{2,1,0:T(8,128)(2,1)}, bf16[8,128,2048]{2,1,0:T(8,128)(2,1)S(1)}, u32[]{:S(2)}) copy-start(bf16[8,128,2048]{2,1,0:T(8,128)(2,1)S(1)} %get-tuple-element.74) | copy-start | bytes 12582916
  184.8 29.5 %copy-start.21 = (bf16[1,128,2048]{2,1,0:T(8,128)(2,1)S(1)}, bf16[1,128,2048]{2,1,0:T(8,128)(2,1)}, u32[]{:S(2)}) copy-start(bf16[1,128,2048]{2,1,0:T(8,128)(2,1)} %param.23) | copy-start | bytes 1572868
  215.0 28.8 %copy-start.10 = (bf16[1024,256]{1,0:T(8,128)(2,1)S(1)}, bf16[1024,256]{1,0:T(8,128)(2,1)}, u32[]{:S(2)}) copy-start(bf16[1024,256]{1,0:T(8,128)(2,1)} %copy-done.9) | copy-start | bytes 1572868
  243.7 1.3 copy-start.14
  245.1 1.9 copy-start.3
  245.1 2.3 copy-start.5
  245.1 2.6 copy-start.12
  290.9 53.7 %copy-start.22 = (f32[44,2048]{1,0:T(8,128)S(1)}, f32[44,2048]{1,0:T(8,128)}, u32[]{:S(2)}) copy-start(f32[44,2048]{1,0:T(8,128)} %param.38) | copy-start | bytes 1081348
  290.9 53.7 %copy-start.24 = (f32[44,2048]{1,0:T(8,128)S(1)}, f32[44,2048]{1,0:T(8,128)}, u32[]{:S(2)}) copy-start(f32[44,2048]{1,0:T(8,128)} %param.39) | copy-start | bytes 1081348
  290.9 53.7 %copy-start.25 = (f32[44,2048]{1,0:T(8,128)S(1)}, f32[44,2048]{1,0:T(8,128)}, u32[]{:S(2)}) copy-start(f32[44,2048]{1,0:T(8,128)} %param.40) | copy-start | bytes 1081348
  290.9 54.9 %copy-start.6 = (f32[16,6144]{1,0:T(8,128)S(1)}, f32[16,6144]{1,0:T(8,128)}, u32[]{:S(2)}) copy-start(f32[16,6144]{1,0:T(8,128)} %refs_0_.3) | copy-start | bytes 1179652
  290.9 54.9 %copy-start.7 = (f32[16,5632]{1,0:T(8,128)S(1)}, f32[16,5632]{1,0:T(8,128)}, u32[]{:S(2)}) copy-start(f32[16,5632]{1,0:T(8,128)} %refs_3_.3) | copy-start | bytes 1081348
  290.9 54.9 %copy-start.8 = (f32[16,5632]{1,0:T(8,128)S(1)}, f32[16,5632]{1,0:T(8,128)}, u32[]{:S(2)}) copy-start(f32[16,5632]{1,0:T(8,128)} %refs_6_.1) | copy-start | bytes 1081348
  290.9 54.8 %copy-start.15 = (f32[16,6144]{1,0:T(8,128)S(1)}, f32[16,6144]{1,0:T(8,128)}, u32[]{:S(2)}) copy-start(f32[16,6144]{1,0:T(8,128)} %refs_1_.1) | copy-start | bytes 1179652
  290.9 54.8 %copy-start.16 = (f32[16,6144]{1,0:T(8,128)S(1)}, f32[16,6144]{1,0:T(8,128)}, u32[]{:S(2)}) copy-start(f32[16,6144]{1,0:T(8,128)} %refs_2_.1) | copy-start | bytes 1179652
  291.0 54.8 %copy-start.17 = (f32[16,5632]{1,0:T(8,128)S(1)}, f32[16,5632]{1,0:T(8,128)}, u32[]{:S(2)}) copy-start(f32[16,5632]{1,0:T(8,128)} %refs_4_.3) | copy-start | bytes 1081348
  291.0 54.8 %copy-start.18 = (f32[16,5632]{1,0:T(8,128)S(1)}, f32[16,5632]{1,0:T(8,128)}, u32[]{:S(2)}) copy-start(f32[16,5632]{1,0:T(8,128)} %refs_5_.1) | copy-start | bytes 1081348
  291.0 54.8 %copy-start.19 = (f32[16,5632]{1,0:T(8,128)S(1)}, f32[16,5632]{1,0:T(8,128)}, u32[]{:S(2)}) copy-start(f32[16,5632]{1,0:T(8,128)} %refs_7_.1) | copy-start | bytes 1081348
  291.0 54.8 %copy-start.20 = (f32[16,5632]{1,0:T(8,128)S(1)}, f32[16,5632]{1,0:T(8,128)}, u32[]{:S(2)}) copy-start(f32[16,5632]{1,0:T(8,128)} %refs_8_.1) | copy-start | bytes 1081348
  338.5 11.9 %copy-start.23 = (f32[16,2048]{1,0:T(8,128)S(1)}, f32[16,2048]{1,0:T(8,128)}, u32[]{:S(2)}) copy-start(f32[16,2048]{1,0:T(8,128)} %param.29) | copy-start | bytes 393220
  338.5 11.9 %copy-start.26 = (f32[16,2048]{1,0:T(8,128)S(1)}, f32[16,2048]{1,0:T(8,128)}, u32[]{:S(2)}) copy-start(f32[16,2048]{1,0:T(8,128)} %param.30) | copy-start | bytes 393220
  338.5 11.9 %copy-start.27 = (f32[16,2048]{1,0:T(8,128)S(1)}, f32[16,2048]{1,0:T(8,128)}, u32[]{:S(2)}) copy-start(f32[16,2048]{1,0:T(8,128)} %param.31) | copy-start | bytes 393220
  338.5 12.7 %copy-start.28 = (f32[7,16]{1,0:T(8,128)S(1)}, f32[7,16]{1,0:T(8,128)}, u32[]{:S(2)}) copy-start(f32[7,16]{1,0:T(8,128)} %param.41) | copy-start | bytes 1348
  338.5 12.7 %copy-start.29 = (f32[7,16]{1,0:T(8,128)S(1)}, f32[7,16]{1,0:T(8,128)}, u32[]{:S(2)}) copy-start(f32[7,16]{1,0:T(8,128)} %param.42) | copy-start | bytes 1348
  338.6 12.7 %copy-start.30 = (f32[7,16]{1,0:T(8,128)S(1)}, f32[7,16]{1,0:T(8,128)}, u32[]{:S(2)}) copy-start(f32[7,16]{1,0:T(8,128)} %param.43) | copy-start | bytes 1348
  338.7 11.7 %collective-permute-start.1 = (bf16[16,2176]{1,0:T(8,128)(2,1)S(1)}, bf16[16,2176]{1,0:T(8,128)(2,1)S(1)}, u32[]{:S(2)}, u32[]{:S(2)}) collective-permute-start(bf16[16,2176]{1,0:T(8,128)(2,1)S(1)} %fusion.5), channel_id=1, source_target_pairs={{0,0},{8,1},{16,2},{24,3},{32,4},{40,5},{48,6},{56,7},{64,8},{72,9... | collective-permute-start | bytes 208904 | tf_op jit(solution)/shard_map/ppermute | solution.py:1500
